TPU v7x, 32 devices: a whole 2x2x4 slice. The times are simulated.
32 devices in a mesh: ens: 2 (over y), band: 16 (over z, x, core).
Axes of the slice: x: 2, y: 2, z: 4, core: 2. Of those that a mesh axis runs over, the one named last changes fastest.
Arguments:
- grid_in: bfloat16 [32768, 256], P(('ens', 'band')), parts along dimension 0, may hold values from -6 to 6
- mesh_state: bfloat16 [8192, 512], P('band'), may hold values from -6 to 6
- enc_owner: int32 [16384, 1], P('band'), may hold values from 0 to 15; in each aligned block of 1024 rows (0 to 1023, 1024 to 2047, ...) at most 128 rows name the same one
- enc_slot: int32 [16384, 1], P('band'), may hold values from 0 to 511
- dec_owner: int32 [16384, 1], P('band'), may hold values from 0 to 15; in each aligned block of 1024 rows (0 to 1023, 1024 to 2047, ...) at most 128 rows name the same one
- dec_slot: int32 [16384, 3], P('band'), may hold values from 0 to 511
- dec_weight: float32 [16384, 3], P('band'), may hold values from 0.2 to 1
- att_list: int32 [64, 4], P('band'), may hold values from 0 to 7, all different within a row
- w_embed: bfloat16 [256, 512], replicated, may hold values from -0.375 to 0.375
- w_message: bfloat16 [512, 512], replicated, may hold values from -0.25 to 0.25
- norm_gain: float32 [3, 512], replicated, may hold values from 0.1 to 1.9
- w_qkv: bfloat16 [1, 512, 1536], replicated, may hold values from -6 to 6
- w_out: bfloat16 [1, 512, 512], replicated, may hold values from -0.25 to 0.25
- w_up: bfloat16 [1, 512, 2048], replicated, may hold values from -0.25 to 0.25
- w_down: bfloat16 [1, 2048, 512], replicated, may hold values from -0.125 to 0.125
- w_dec1: bfloat16 [512, 512], replicated, may hold values from -0.25 to 0.25
- w_dec2: bfloat16 [512, 84], replicated, may hold values from -0.25 to 0.25
Outputs:
- denoised: bfloat16 [84, 32768], P(None, ('ens', 'band')), parts along dimension 1
There are 2 independent parts, one for each index of `ens`. A program takes and returns all parts, laid end to end along the dimension named above; an argument that names none is the same for every part. Nothing has to cross between parts.
Inputs may be any that keep to these rules, and one draw needn't show every extreme that they name: `enc_owner`: in the rows of one band (aligned blocks of 1024 rows) no mesh shard is named by more than 128 rows. `dec_owner`: in the rows of one band (aligned blocks of 1024 rows) no mesh shard is named by more than 128 rows. `att_list`: each row names 4 different window blocks.
All inputs are finite; a program needn't handle non-finite values.
Results may differ from a plain program's by a relative error of at most 0.014.
Values may be sent and summed in bfloat16 or wider, within the bound.
No kernel may reach another device: no remote copies, remote signals or barrier semaphores. Data moves between devices by JAX's collectives and lax.ppermute only.
A program may use at most 128 MiB of HBM per device.

v0:
```python
import jax
import jax.numpy as jnp
from jax import lax
from jax.sharding import PartitionSpec as P

HEADS = 4
BLK = 128
NB = 4


epsilon = 1e-05


def extended(x, sides, width):
    for axis, dim in sides:
        peers, length = (lax.axis_size(axis), x.shape[dim])
        up = [(i, (i + 1) % peers) for i in range(peers - 1)]
        down = [(j, i) for i, j in up]
        last = lax.slice_in_dim(x, length - width, length, axis=dim)
        first = lax.slice_in_dim(x, 0, width, axis=dim)
        before = lax.ppermute(last, axis, up)
        after = lax.ppermute(first, axis, down)
        x = jnp.concatenate([before, x, after], axis=dim)
    return x


def layer_norm(values, gains):
    average = jnp.mean(values, axis=-1, keepdims=True)
    centred = values - average
    spread_sq = jnp.mean(centred * centred, axis=-1, keepdims=True)
    return centred * lax.rsqrt(spread_sq + epsilon) * gains


def bucket_positions(owners, peer_count):
    onehot = (owners[:, None] == jnp.arange(peer_count, dtype=jnp.int32)[None, :]).astype(jnp.int32)
    ranking = jnp.cumsum(onehot, axis=0) - 1
    return jnp.sum(onehot * ranking, axis=1)


def attend(projected, side_kv, att_list, band_pos, peer_count):
    mesh_rows = projected.shape[0]
    model_width = projected.shape[1] // 3
    head_size = model_width // HEADS
    blocks = mesh_rows // BLK
    scaling = head_size ** (-0.5)
    own_part = projected.reshape(mesh_rows, 3, HEADS, head_size)
    window = side_kv.reshape(2 * blocks, BLK, 2, HEADS, head_size)
    chosen = window[att_list].reshape(blocks, NB * BLK, 2, HEADS, head_size)
    usable = jnp.where(att_list < blocks, band_pos > 0, band_pos < peer_count - 1)
    usable = jnp.repeat(usable, BLK, axis=1)
    queries = own_part[:, 0]
    local_scores = (
        jnp.einsum("qhd,khd->hqk", queries, own_part[:, 1], preferred_element_type=jnp.float32)
        * scaling
    )
    local_scores = local_scores.reshape(HEADS, blocks, BLK, mesh_rows)
    remote_scores = (
        jnp.einsum(
            "bqhd,bkhd->hbqk",
            queries.reshape(blocks, BLK, HEADS, head_size),
            chosen[:, :, 0],
            preferred_element_type=jnp.float32,
        )
        * scaling
    )
    remote_scores = jnp.where(usable[None, :, None, :], remote_scores, -jnp.inf)
    highest = jnp.maximum(jnp.max(local_scores, axis=-1), jnp.max(remote_scores, axis=-1))
    local_probs = jnp.exp(local_scores - highest[..., None])
    remote_probs = jnp.exp(remote_scores - highest[..., None])
    totals = jnp.sum(local_probs, axis=-1) + jnp.sum(remote_probs, axis=-1)
    combined = jnp.einsum(
        "hbqk,khd->bqhd",
        local_probs.astype(jnp.bfloat16),
        own_part[:, 2],
        preferred_element_type=jnp.float32,
    )
    combined = combined + jnp.einsum(
        "hbqk,bkhd->bqhd",
        remote_probs.astype(jnp.bfloat16),
        chosen[:, :, 1],
        preferred_element_type=jnp.float32,
    )
    combined = combined / jnp.transpose(totals, (1, 2, 0))[..., None]
    return combined.reshape(mesh_rows, model_width).astype(jnp.bfloat16)


def body(
    grid_in,
    mesh_state,
    enc_owner,
    enc_slot,
    dec_owner,
    dec_slot,
    dec_weight,
    att_list,
    w_embed,
    w_message,
    norm_gain,
    w_qkv,
    w_out,
    w_up,
    w_down,
    w_dec1,
    w_dec2,
):
    peer_count = lax.axis_size("band")
    band_pos = lax.axis_index("band")
    grid_rows = grid_in.shape[0]
    mesh_rows = mesh_state.shape[0]
    model_width = mesh_state.shape[1]
    capacity = 2 * grid_rows // peer_count
    grid_latent = jax.nn.silu(jnp.dot(grid_in, w_embed, preferred_element_type=jnp.float32)).astype(
        jnp.bfloat16
    )
    enc_owners = enc_owner[:, 0]
    placed = enc_owners * capacity + bucket_positions(enc_owners, peer_count)
    slot_out = (
        jnp.full((peer_count * capacity,), mesh_rows, jnp.int32)
        .at[placed]
        .set(enc_slot[:, 0])
        .reshape(peer_count, capacity)
    )
    message = jnp.dot(grid_latent, w_message, preferred_element_type=jnp.float32).astype(
        jnp.bfloat16
    )
    rows_out = (
        jnp.zeros((peer_count * capacity, model_width), jnp.bfloat16)
        .at[placed]
        .set(message)
        .reshape(peer_count, capacity, model_width)
    )
    arrived, arrived_slots = (
        lax.all_to_all(rows_out, "band", split_axis=0, concat_axis=0, tiled=True),
        lax.all_to_all(slot_out, "band", split_axis=0, concat_axis=0, tiled=True),
    )
    incoming = (
        jnp.zeros((mesh_rows + 1, model_width), jnp.float32)
        .at[arrived_slots.reshape(-1)]
        .add(arrived.reshape(-1, model_width).astype(jnp.float32))
    )
    stream = mesh_state.astype(jnp.float32) + incoming[:mesh_rows]
    layers = w_qkv.shape[0]
    normed = layer_norm(stream, norm_gain[0]).astype(jnp.bfloat16)
    projected = jnp.dot(normed, w_qkv[0], preferred_element_type=jnp.float32).astype(jnp.bfloat16)
    neighbours = extended(projected[:, model_width:], (("band", 0),), mesh_rows)
    side_kv = jnp.concatenate([neighbours[:mesh_rows], neighbours[2 * mesh_rows :]], axis=0)
    attended = attend(projected, side_kv, att_list, band_pos, peer_count)
    stream = stream + jnp.dot(attended, w_out[0], preferred_element_type=jnp.float32)
    normed = layer_norm(stream, norm_gain[1]).astype(jnp.bfloat16)
    hidden = jax.nn.silu(jnp.dot(normed, w_up[0], preferred_element_type=jnp.float32)).astype(
        jnp.bfloat16
    )
    stream = stream + jnp.dot(hidden, w_down[0], preferred_element_type=jnp.float32)
    final = layer_norm(stream, norm_gain[2 * layers]).astype(jnp.bfloat16)
    dec_owners = dec_owner[:, 0]
    dec_placed = dec_owners * capacity + bucket_positions(dec_owners, peer_count)
    requests = (
        jnp.zeros((peer_count * capacity, 3), jnp.int32)
        .at[dec_placed]
        .set(dec_slot)
        .reshape(peer_count, capacity, 3)
    )
    edge_weights = (
        jnp.zeros((peer_count * capacity, 3), jnp.float32)
        .at[dec_placed]
        .set(dec_weight)
        .reshape(peer_count, capacity, 3)
    )
    slot_ids = lax.all_to_all(requests, "band", split_axis=0, concat_axis=0, tiled=True)
    scaled = lax.all_to_all(edge_weights, "band", split_axis=0, concat_axis=0, tiled=True)
    row_data = final[slot_ids].astype(jnp.float32)
    summed = jnp.sum(scaled[..., None] * row_data, axis=2).astype(jnp.bfloat16)
    returned = lax.all_to_all(summed, "band", split_axis=0, concat_axis=0, tiled=True)
    pulled = returned.reshape(peer_count * capacity, model_width)[dec_placed]
    mixed = (grid_latent.astype(jnp.float32) + pulled.astype(jnp.float32)).astype(jnp.bfloat16)
    decoded = jax.nn.silu(jnp.dot(mixed, w_dec1, preferred_element_type=jnp.float32)).astype(
        jnp.bfloat16
    )
    result = lax.dot_general(
        w_dec2, decoded, (((0,), (1,)), ((), ())), preferred_element_type=jnp.float32
    )
    return result.astype(jnp.bfloat16)


def solution(mesh):
    return jax.shard_map(
        body,
        mesh=mesh,
        in_specs=(
            P(("ens", "band"), None),
            P("band", None),
            P("band", None),
            P("band", None),
            P("band", None),
            P("band", None),
            P("band", None),
            P("band", None),
            P(),
            P(),
            P(),
            P(),
            P(),
            P(),
            P(),
            P(),
            P(),
        ),
        out_specs=P(None, ("ens", "band")),
        check_vma=False,
    )
```

profile of v0, /device:TPU:11, one launch (start us, length us, event | category | flops | bytes accessed | tf_op | source)
XLA Modules:
  0.0 312.7 jit_solution(7186750906810702678)
XLA Ops:
  0.8 4.5 %reduce-window.16 = s32[16,8,128]{2,1,0:T(8,128)S(1)} reduce-window(s32[16,8,128]{2,1,0:T(8,128)S(1)} %fusion.65, s32[]{:T(128)} %constant.20.clone.1), window={size=1x1x128 pad=0_0x0_0x127_0}, to_apply=%region_4.5 | reduce-window | flops 2080768 | bytes 131076 | tf_op jit(solution)/shard_map/reduce-window.2
  7.2 5.0 %scatter_custom_fusion.1 = s32[2048]{0:T(1024)} fusion(s32[1024]{0:T(1024)S(1)} %bitcast.169, s32[1024]{0:T(1024)} %bitcast.173, s32[]{:T(128)} %constant.23.clone.1), kind=kCustom, calls=%fused_computation.103 | custom fusion | bytes 8704 | tf_op jit(solution)/shard_map/scatter | solution.py:120
  12.2 6.6 %all-to-all-start.1 = ((s32[16,1,128]{2,1,0:T(1,128)}), s32[16,1,128]{2,1,0:T(1,128)S(1)}, u32[]{:S(2)}, u32[]{:S(2)}) async-start(s32[16,1,128]{2,1,0:T(1,128)} %bitcast.14), calls=%async_computation.1 | async-start | bytes 16384 | tf_op jit(solution)/shard_map/all_to_all | solution.py:134
  23.4 7.2 %scatter_custom_fusion.2 = bf16[2048,512]{1,0:T(8,128)(2,1)} fusion(s32[1024]{0:T(1024)S(1)} %bitcast.170, bf16[1024,512]{1,0:T(8,128)(2,1)} %convolution_convert_fusion.1, bf16[]{:T(256)} %constant.25.clone.1), kind=kCustom, calls=%fused_computation.57 | custom fusion | bytes 2097664 | tf_op jit(solution)/shard_map/scatter | solution.py:129
  30.6 6.2 %all-to-all-start.2 = ((bf16[16,128,512]{2,1,0:T(8,128)(2,1)}), bf16[16,128,512]{2,1,0:T(8,128)(2,1)}, u32[]{:S(2)}, u32[]{:S(2)}) async-start(bf16[16,128,512]{2,1,0:T(8,128)(2,1)} %bitcast.145), calls=%async_computation.2 | async-start | bytes 4194304 | tf_op jit(solution)/shard_map/all_to_all | solution.py:133
  38.0 4.5 %reduce-window.14 = s32[16,8,128]{2,1,0:T(8,128)S(1)} reduce-window(s32[16,8,128]{2,1,0:T(8,128)S(1)} %fusion.64, s32[]{:T(128)} %constant.20.clone.1), window={size=1x1x128 pad=0_0x0_0x127_0}, to_apply=%region_0.1 | reduce-window | flops 2080768 | bytes 131076 | tf_op jit(solution)/shard_map/reduce-window
  44.0 3.7 %scatter_custom_fusion.4 = s32[2048,3]{1,0:T(8,128)S(1)} fusion(s32[1024]{0:T(1024)S(1)} %bitcast.164, s32[1024,3]{1,0:T(8,128)} %copy.63, s32[]{:T(128)} %constant.20.clone.1), kind=kCustom, calls=%fused_computation.68 | custom fusion | bytes 25088 | tf_op jit(solution)/shard_map/scatter | solution.py:160
  49.8 3.7 %scatter_custom_fusion = f32[2048,3]{1,0:T(8,128)S(1)} fusion(s32[1024]{0:T(1024)S(1)} %bitcast.165, f32[1024,3]{1,0:T(8,128)} %copy.50, f32[]{:T(128)} %constant.18.clone.1), kind=kCustom, calls=%fused_computation.76 | custom fusion | bytes 25088 | tf_op jit(solution)/shard_map/scatter | solution.py:166
  54.5 29.8 %all-to-all-done.2 = bf16[16,128,512]{2,1,0:T(8,128)(2,1)} async-done(((bf16[16,128,512]{2,1,0:T(8,128)(2,1)}), bf16[16,128,512]{2,1,0:T(8,128)(2,1)}, u32[]{:S(2)}, u32[]{:S(2)}) %all-to-all-start.2) | async-done | bytes 2097184 | tf_op jit(solution)/shard_map/all_to_all | solution.py:133
  84.3 4.9 %all-to-all-start.3 = ((s32[16,128,3]{1,2,0:T(4,128)}), s32[16,128,3]{1,2,0:T(4,128)S(1)}, u32[]{:S(2)}, u32[]{:S(2)}) async-start(s32[16,128,3]{1,2,0:T(4,128)} %copy.64), calls=%async_computation.3 | async-start | bytes 65536 | tf_op jit(solution)/shard_map/all_to_all | solution.py:169
  89.2 14.9 %scatter_custom_fusion.3 = f32[513,512]{1,0:T(8,128)S(1)} fusion(s32[2048]{0:T(1024)S(1)} %bitcast.168, bf16[2048,512]{1,0:T(8,128)(2,1)} %bitcast.42, f32[]{:T(128)} %constant.18.clone.1), kind=kCustom, calls=%fused_computation.9 | custom fusion | flops 2097152 | bytes 3147780 | tf_op jit(solution)/shard_map/scatter-add | solution.py:139
  118.2 6.2 %all-to-all-start = ((f32[16,128,3]{1,2,0:T(4,128)}), f32[16,128,3]{1,2,0:T(4,128)S(1)}, u32[]{:S(2)}, u32[]{:S(2)}) async-start(f32[16,128,3]{1,2,0:T(4,128)} %copy.51), calls=%async_computation | async-start | bytes 65536 | tf_op jit(solution)/shard_map/all_to_all | solution.py:170
  127.6 13.1 %all-to-all-done = f32[16,128,3]{1,2,0:T(4,128)S(1)} async-done(((f32[16,128,3]{1,2,0:T(4,128)}), f32[16,128,3]{1,2,0:T(4,128)S(1)}, u32[]{:S(2)}, u32[]{:S(2)}) %all-to-all-start) | async-done | bytes 24608 | tf_op jit(solution)/shard_map/all_to_all | solution.py:170
  142.1 4.0 %reshape.160 = bf16[512,3,4,128]{3,2,1,0:T(4,128)(2,1)} reshape(bf16[512,1536]{1,0:T(8,128)(2,1)} %copy-done.4) | data formatting | bytes 3145728 | tf_op jit(solution)/shard_map/reshape | solution.py:46
  157.5 4.5 %reshape.162 = bf16[8,128,2,4,128]{4,3,2,1,0:T(4,128)(2,1)} reshape(bf16[1024,1024]{1,0:T(8,128)(2,1)} %pad_maximum_fusion) | data formatting | bytes 4194304 | tf_op jit(solution)/shard_map/reshape | solution.py:47
  161.9 7.1 %gather_fusion = bf16[16,128,2,4,128]{4,3,2,1,0:T(4,128)(2,1)} fusion(bf16[8,128,2,4,128]{4,3,2,1,0:T(4,128)(2,1)} %reshape.162, s32[1024]{0:T(1024)S(1)} %pad_clamp_fusion), kind=kCustom, calls=%fused_computation | custom fusion | bytes 8388672 | tf_op jit(solution)/shard_map/gather | solution.py:48
  178.1 4.5 %fusion.34 = bf16[4,128,4,128]{1,3,0,2:T(8,128)(2,1)} fusion(f32[4,128,4,128]{1,3,0,2:T(8,128)} %fusion.25, f32[4,4,128,512]{3,2,1,0:T(8,128)} %bitcast.142, f32[4,4,128]{2,1,0:T(4,128)S(1)} %max.10, bf16[512,1,4,128]{0,3,2,1:T(8,128)(2,1)} %copy.70, f32[4,128,4]{1,0,2:T(4,128)S(1)} %add_bitcast_fusion), kind=kOutput, calls=%fused_computation.47 | convolution fusion | flops 271319040 | bytes 6307840 | tf_op jit(solution)/shard_map/hbqk,khd->bqhd/dot_general | solution.py:71
  187.8 5.1 %fusion.77 = (f32[512]{0:T(512)S(1)}, f32[512,512]{0,1:T(8,128)S(1)}) fusion(f32[512,512]{0,1:T(8,128)} %copy-done.6, bf16[1,2048,512]{2,1,0:T(8,128)(2,1)S(1)} %copy-done, bf16[1,512,2048]{2,1,0:T(8,128)(2,1)} %param.30, f32[512]{0:T(512)S(1)} %bitcast.171, f32[512]{0:T(512)S(1)} %add_rsqrt_fusion.1, f32[512]{0:T(512)S(1)} %broadcast_multiply_fusion.1), kind=kOutput, calls=%fused_computation.123 | convolution fusion | flops 2154298880 | bytes 6299648 | tf_op jit(solution)/shard_map/dot_general | solution.py:153
  193.4 25.4 %gather_fusion.1 = bf16[6144,512]{1,0:T(8,128)(2,1)} fusion(bf16[512,512]{1,0:T(8,128)(2,1)S(1)} %copy.66, s32[6144]{0:T(1024)S(1)} %broadcast_clamp_fusion), kind=kCustom, calls=%fused_computation.1 | custom fusion | bytes 12607488 | tf_op jit(solution)/shard_map/gather | solution.py:171
  218.8 18.1 %reshape.236 = f32[16,128,3,512]{3,2,1,0:T(4,128)} reshape(bf16[6144,512]{1,0:T(8,128)(2,1)} %gather_fusion.1) | data formatting | bytes 18874368 | tf_op jit(solution)/shard_map/convert_element_type | solution.py:171
  236.9 15.0 %multiply_reduce_fusion = bf16[16,128,512]{2,1,0:T(8,128)(2,1)} fusion(f32[16,128,3,512]{3,2,1,0:T(4,128)} %reshape.236, f32[16,128,3]{2,1,0:T(8,128)S(1)} %copy-done.5), kind=kLoop, calls=%fused_computation.8 | loop fusion | flops 5242880 | bytes 14704640 | tf_op jit(solution)/shard_map/reduce_sum | solution.py:172
  251.9 5.9 %all-to-all-start.4 = ((bf16[16,128,512]{2,1,0:T(8,128)(2,1)}), bf16[16,128,512]{2,1,0:T(8,128)(2,1)S(1)}, u32[]{:S(2)}, u32[]{:S(2)}) async-start(bf16[16,128,512]{2,1,0:T(8,128)(2,1)} %multiply_reduce_fusion), calls=%async_computation.4 | async-start | bytes 4194304 | tf_op jit(solution)/shard_map/all_to_all | solution.py:173
  257.8 47.4 %all-to-all-done.4 = bf16[16,128,512]{2,1,0:T(8,128)(2,1)S(1)} async-done(((bf16[16,128,512]{2,1,0:T(8,128)(2,1)}), bf16[16,128,512]{2,1,0:T(8,128)(2,1)S(1)}, u32[]{:S(2)}, u32[]{:S(2)}) %all-to-all-start.4) | async-done | bytes 2097184 | tf_op jit(solution)/shard_map/all_to_all | solution.py:173
  305.2 4.0 %gather_fusion.2 = bf16[1024,512]{1,0:T(8,128)(2,1)S(1)} fusion(bf16[2048,512]{1,0:T(8,128)(2,1)S(1)} %bitcast.141, s32[1024]{0:T(1024)S(1)} %broadcast_clamp_fusion.1), kind=kCustom, calls=%fused_computation.2 | custom fusion | bytes 2101248 | tf_op jit(solution)/shard_map/gather | solution.py:174
  (115 shorter events, 61.1 us)
Async XLA Ops:
  0.0 187.7 %copy-start = (bf16[1,2048,512]{2,1,0:T(8,128)(2,1)S(1)}, bf16[1,2048,512]{2,1,0:T(8,128)(2,1)}, u32[]{:S(2)}) copy-start(bf16[1,2048,512]{2,1,0:T(8,128)(2,1)} %param.31) | copy-start | bytes 6291460
  12.2 18.3 %all-to-all-start.1 = ((s32[16,1,128]{2,1,0:T(1,128)}), s32[16,1,128]{2,1,0:T(1,128)S(1)}, u32[]{:S(2)}, u32[]{:S(2)}) async-start(s32[16,1,128]{2,1,0:T(1,128)} %bitcast.14), calls=%async_computation.1 | async-start | bytes 16384 | tf_op jit(solution)/shard_map/all_to_all | solution.py:134
  18.8 2.9 copy-start.15
  20.7 1.0 copy-start.17
  30.6 6.2 %copy-start.8 = (bf16[512,512]{1,0:T(8,128)(2,1)S(1)}, bf16[512,512]{1,0:T(8,128)(2,1)}, u32[]{:S(2)}) copy-start(bf16[512,512]{1,0:T(8,128)(2,1)} %param.18) | copy-start | bytes 1572868
  30.6 7.3 %copy-start.12 = (s32[4,4]{1,0:T(4,128)S(1)}, s32[4,4]{1,0:T(4,128)}, u32[]{:S(2)}) copy-start(s32[4,4]{1,0:T(4,128)} %param.24) | copy-start | bytes 196
  30.6 7.4 %copy-start.9 = (s32[1024,1]{0,1:T(1,128)S(1)}, s32[1024,1]{0,1:T(1,128)}, u32[]{:S(2)}) copy-start(s32[1024,1]{0,1:T(1,128)} %param.21) | copy-start | bytes 12292
  30.6 12.3 %copy-start.10 = (s32[1024,3]{0,1:T(4,128)S(1)}, s32[1024,3]{0,1:T(4,128)}, u32[]{:S(2)}) copy-start(s32[1024,3]{0,1:T(4,128)} %param.22) | copy-start | bytes 36868
  30.6 53.7 %all-to-all-start.2 = ((bf16[16,128,512]{2,1,0:T(8,128)(2,1)}), bf16[16,128,512]{2,1,0:T(8,128)(2,1)}, u32[]{:S(2)}, u32[]{:S(2)}) async-start(bf16[16,128,512]{2,1,0:T(8,128)(2,1)} %bitcast.145), calls=%async_computation.2 | async-start | bytes 4194304 | tf_op jit(solution)/shard_map/all_to_all | solution.py:133
  36.8 12.0 %copy-start.11 = (f32[1024,3]{0,1:T(4,128)S(1)}, f32[1024,3]{0,1:T(4,128)}, u32[]{:S(2)}) copy-start(f32[1024,3]{0,1:T(4,128)} %param.23) | copy-start | bytes 36868
  47.8 6.7 %copy-start.13 = (f32[3,512]{1,0:T(4,128)S(1)}, f32[3,512]{1,0:T(4,128)}, u32[]{:S(2)}) copy-start(f32[3,512]{1,0:T(4,128)} %param.27) | copy-start | bytes 18436
  84.3 33.9 %all-to-all-start.3 = ((s32[16,128,3]{1,2,0:T(4,128)}), s32[16,128,3]{1,2,0:T(4,128)S(1)}, u32[]{:S(2)}, u32[]{:S(2)}) async-start(s32[16,128,3]{1,2,0:T(4,128)} %copy.64), calls=%async_computation.3 | async-start | bytes 65536 | tf_op jit(solution)/shard_map/all_to_all | solution.py:169
  106.7 2.6 copy-start.3
  106.7 2.6 copy-start.14
  110.5 1.2 copy-start.4
  112.7 41.7 %collective-permute-start = (bf16[512,1024]{1,0:T(8,128)(2,1)}, bf16[512,1024]{1,0:T(8,128)(2,1)}, u32[]{:S(2)}, u32[]{:S(2)}) collective-permute-start(bf16[512,1024]{1,0:T(8,128)(2,1)} %slice.70), channel_id=1, source_target_pairs={{0,1},{1,2},{2,3},{3,4},{4,5},{5,6},{6,7},{7,8},{8,9},{9,10},{10,1... | collective-permute-start | bytes 3145736 | tf_op jit(solution)/shard_map/ppermute | solution.py:21
  116.2 38.2 %collective-permute-start.1 = (bf16[512,1024]{1,0:T(8,128)(2,1)}, bf16[512,1024]{1,0:T(8,128)(2,1)}, u32[]{:S(2)}, u32[]{:S(2)}) collective-permute-start(bf16[512,1024]{1,0:T(8,128)(2,1)} %slice.70), channel_id=1, source_target_pairs={{1,0},{2,1},{3,2},{4,3},{5,4},{6,5},{7,6},{8,7},{9,8},{10,9},{11,1... | collective-permute-start | bytes 3145736 | tf_op jit(solution)/shard_map/ppermute | solution.py:22
  118.2 22.6 %all-to-all-start = ((f32[16,128,3]{1,2,0:T(4,128)}), f32[16,128,3]{1,2,0:T(4,128)S(1)}, u32[]{:S(2)}, u32[]{:S(2)}) async-start(f32[16,128,3]{1,2,0:T(4,128)} %copy.51), calls=%async_computation | async-start | bytes 65536 | tf_op jit(solution)/shard_map/all_to_all | solution.py:170
  169.0 3.3 %copy-start.7 = (bf16[512,1,4,128]{3,0,2,1:T(8,128)(2,1)S(1)}, bf16[512,1,4,128]{3,0,2,1:T(8,128)(2,1)}, u32[]{:S(2)}) copy-start(bf16[512,1,4,128]{3,0,2,1:T(8,128)(2,1)} %copy.71) | copy-start | bytes 1572868
  174.5 2.5 copy-start.2
  218.8 18.1 %copy-start.5 = (f32[16,128,3]{2,1,0:T(8,128)S(1)}, f32[16,128,3]{2,1,0:T(8,128)}, u32[]{:S(2)}) copy-start(f32[16,128,3]{2,1,0:T(8,128)} %copy.52) | copy-start | bytes 73732
  251.9 53.3 %all-to-all-start.4 = ((bf16[16,128,512]{2,1,0:T(8,128)(2,1)}), bf16[16,128,512]{2,1,0:T(8,128)(2,1)S(1)}, u32[]{:S(2)}, u32[]{:S(2)}) async-start(bf16[16,128,512]{2,1,0:T(8,128)(2,1)} %multiply_reduce_fusion), calls=%async_computation.4 | async-start | bytes 4194304 | tf_op jit(solution)/shard_map/all_to_all | solution.py:173
  305.2 4.0 %copy-start.16 = (bf16[512,84]{0,1:T(8,128)(2,1)S(1)}, bf16[512,84]{0,1:T(8,128)(2,1)}, u32[]{:S(2)}) copy-start(bf16[512,84]{0,1:T(8,128)(2,1)} %param.33) | copy-start | bytes 258052
  309.2 3.4 %copy-start.1 = (bf16[1,2048,512]{2,1,0:T(8,128)(2,1)S(1)}, bf16[1,2048,512]{2,1,0:T(8,128)(2,1)}, u32[]{:S(2)}) copy-start(bf16[1,2048,512]{2,1,0:T(8,128)(2,1)} %param.31) | copy-start | bytes 6291460
  (1 other events, 1.0 us)
where the time goes:
time: 314 us; the launch traced here: 313 us
  local copies, waits for them, and re-layouts  111 us (35%)
  waiting for transfers between devices  90.4 us (29%)
  other arithmetic  50.1 us (16%)
  starting transfers between devices  35.1 us (11%)
  matrix products  25.5 us (8%)
    all_to_all x1, waiting for transfers between devices, body(): lax.all_to_all(summed, 'band', split_axis=0, concat_axis=0, tiled=True)  47.4 us
    all_to_all x1, waiting for transfers between devices, body(): lax.all_to_all(rows_out, 'band', split_axis=0, concat_axis=0, tiled=True)  29.8 us
    gather x1, local copies, waits for them, and re-layouts, body(): row_data = final[slot_ids].astype(jnp.float32)  25.4 us
    convert_element_type x1, local copies, waits for them, and re-layouts, body(): row_data = final[slot_ids].astype(jnp.float32)  18.1 us
    reduce_sum x1, other arithmetic, body(): summed = jnp.sum(scaled[..., None] * row_data, axis=2).astype(jnp.bfloat16)  15 us
    scatter-add x1, other arithmetic, body(): incoming = jnp.zeros((mesh_rows + 1, model_width), jnp.float32).at[arrive...  14.9 us
    all_to_all x1, waiting for transfers between devices, body(): lax.all_to_all(edge_weights, 'band', split_axis=0, concat_axis=0, tiled=T...  13.1 us
    unnamed x44, local copies, waits for them, and re-layouts  10.9 us
  transfers between devices with their start and end apart: 7, of which 3 were waited for; matrix products, arithmetic and copies ran while one was open for 22% of the time, Pallas kernels for 0%

commit v1 on v0

v1 whole, which is shorter than its diff:
```python
import functools

import jax
import jax.numpy as jnp
from jax import lax
from jax.experimental import pallas as pl
from jax.experimental.pallas import tpu as pltpu
from jax.sharding import PartitionSpec as P

HEADS = 4
BLK = 128
NB = 4
META = 16
ROWS = 512
RET = 96
LOW = 32
MASKED = -1e30
VMEM_LIMIT = 40 * 1024 * 1024

epsilon = 1e-05

F32 = jnp.float32
BF16 = jnp.bfloat16


def dot(a, b):
    return jnp.dot(a, b, preferred_element_type=F32)


def dot_nt(a, b):
    return lax.dot_general(a, b, (((1,), (1,)), ((), ())), preferred_element_type=F32)


def silu(v):
    return v / (1.0 + jnp.exp(-v))


def layer_norm(values, gains):
    average = jnp.mean(values, axis=-1, keepdims=True)
    centred = values - average
    spread_sq = jnp.mean(centred * centred, axis=-1, keepdims=True)
    return centred * lax.rsqrt(spread_sq + epsilon) * gains


def call(kernel, out_shape, args, scratch=(), smem=(), flops=0, moved=0):
    specs = [
        pl.BlockSpec(memory_space=pltpu.SMEM if i in smem else pltpu.VMEM)
        for i in range(len(args))
    ]
    outs = jax.tree.map(lambda _: pl.BlockSpec(memory_space=pltpu.VMEM), out_shape)
    return pl.pallas_call(
        kernel,
        out_shape=out_shape,
        in_specs=specs,
        out_specs=outs,
        scratch_shapes=list(scratch),
        compiler_params=pltpu.CompilerParams(vmem_limit_bytes=VMEM_LIMIT),
        cost_estimate=pl.CostEstimate(flops=flops, bytes_accessed=moved, transcendentals=0),
    )(*args)


def owner_onehot(owner, peers):
    places = lax.broadcasted_iota(jnp.int32, (peers, owner.shape[1]), 0)
    return jnp.where(places == owner, 1.0, 0.0).astype(F32)


def rank_onehot(rank, cap):
    places = lax.broadcasted_iota(jnp.int32, (cap, rank.shape[1]), 0).astype(F32)
    return jnp.where(places == rank, 1.0, 0.0).astype(BF16)


def bucket_kernel(peers, cap, weighted, *refs):
    if weighted:
        owner_ref, slot_ref, weight_ref, rows_ref, out_ref, rank_ref = refs
    else:
        owner_ref, slot_ref, rows_ref, out_ref, rank_ref = refs
    grid, width = rows_ref.shape
    part = 256 if grid % 256 == 0 else grid
    chosen = owner_onehot(owner_ref[...], peers)
    chosen16 = chosen.astype(BF16)
    upto = jnp.where(
        lax.broadcasted_iota(jnp.int32, (part, part), 0)
        <= lax.broadcasted_iota(jnp.int32, (part, part), 1),
        1.0,
        0.0,
    ).astype(BF16)
    carry = jnp.zeros((peers, 1), F32)
    ranks = []
    for c in range(grid // part):
        span = slice(c * part, (c + 1) * part)
        counts = dot(chosen16[:, span], upto) + carry
        carry = counts[:, part - 1 :]
        ranks.append(jnp.sum(chosen[:, span] * counts, axis=0, keepdims=True) - 1.0)
    rank = jnp.concatenate(ranks, axis=1)
    rank_ref[...] = rank
    placed = rank_onehot(rank, cap)

    slots = slot_ref[...]
    pieces = [(slots // LOW).astype(F32), (slots % LOW).astype(F32)]
    if weighted:
        weights = weight_ref[...]
        upper = weights.astype(BF16).astype(F32)
        pieces += [upper, weights - upper]
    held = sum(p.shape[0] for p in pieces)
    pieces.append(jnp.zeros((META - held, grid), F32))
    features = jnp.concatenate(pieces, axis=0).astype(BF16).astype(F32)
    spread = (chosen[:, None, :] * features[None, :, :]).reshape(peers * META, grid)
    meta = dot_nt(spread.astype(BF16), placed).reshape(peers, META, cap)
    out_ref[:, cap:, :] = jnp.zeros((peers, META, width), BF16)
    out_ref[:, cap:, :cap] = meta.astype(BF16)

    rows = rows_ref[...]
    step = ROWS // cap
    for o in range(0, peers, step):
        select = (chosen16[o : o + step, None, :] * placed[None, :, :]).reshape(step * cap, grid)
        moved = dot(select, rows)
        out_ref[o : o + step, :cap, :] = moved.astype(BF16).reshape(step, cap, width)


def bucket(owner, slots, weights, rows, peers, cap):
    grid, width = rows.shape
    weighted = weights is not None
    args = (owner, slots) + ((weights,) if weighted else ()) + (rows,)
    return call(
        functools.partial(bucket_kernel, peers, cap, weighted),
        (
            jax.ShapeDtypeStruct((peers, cap + META, width), BF16),
            jax.ShapeDtypeStruct((1, grid), F32),
        ),
        args,
        flops=2 * peers * cap * grid * width,
        moved=2 * (grid * width + peers * (cap + META) * width),
    )


def slot_row(got_ref, o, step, cap, low, count):
    def piece(r):
        rows = got_ref[r, cap:, :cap].astype(F32)
        upper = rows[low : low + 1, :]
        lower = rows[low + count : low + count + 1, :]
        return upper * LOW + lower

    return jnp.concatenate([piece(r) for r in range(o, o + step)], axis=1)


def weight_row(got_ref, o, step, cap, first):
    def piece(r):
        rows = got_ref[r, cap:, :cap].astype(F32)
        return rows[first : first + 1, :] + rows[first + 3 : first + 4, :]

    return jnp.concatenate([piece(r) for r in range(o, o + step)], axis=1)


def encode_kernel(peers, cap, got_ref, state_ref, embed_ref, message_ref, gain_ref, stream_ref, normed_ref):
    width = got_ref.shape[2]
    nodes = state_ref.shape[0]
    step = ROWS // cap
    stream_ref[...] = state_ref[...].astype(F32)
    for o in range(0, peers, step):
        rows = got_ref[o : o + step, :cap, :].reshape(ROWS, width)
        latent = silu(dot(rows, embed_ref[...])).astype(BF16)
        message = dot(latent, message_ref[...]).astype(BF16)
        slot = slot_row(got_ref, o, step, cap, 0, 1)
        places = lax.broadcasted_iota(jnp.int32, (nodes, ROWS), 0).astype(F32)
        target = jnp.where(places == slot, 1.0, 0.0).astype(BF16)
        stream_ref[...] += dot(target, message)
    normed_ref[...] = layer_norm(stream_ref[...], gain_ref[0:1, :]).astype(BF16)


def local_kernel(normed_ref, qkv_ref, query_ref, partial_ref, stats_ref):
    nodes, width = normed_ref.shape
    head = width // HEADS
    scaling = head ** (-0.5)
    normed = normed_ref[...]
    query = dot(normed, qkv_ref[:, :width]).astype(BF16)
    key = dot(normed, qkv_ref[:, width : 2 * width]).astype(BF16)
    value = dot(normed, qkv_ref[:, 2 * width :]).astype(BF16)
    query_ref[...] = query
    stats = []
    for h in range(HEADS):
        cols = slice(h * head, (h + 1) * head)
        scores = dot_nt(query[:, cols], key[:, cols]) * scaling
        highest = jnp.max(scores, axis=-1, keepdims=True)
        probs = jnp.exp(scores - highest)
        stats += [highest, jnp.sum(probs, axis=-1, keepdims=True)]
        partial_ref[:, cols] = dot(probs.astype(BF16), value[:, cols])
    lanes = lax.broadcasted_iota(jnp.int32, (nodes, BLK), 1)
    packed = jnp.zeros((nodes, BLK), F32)
    for i, s in enumerate(stats):
        packed = jnp.where(lanes == i, s, packed)
    stats_ref[...] = packed


def mesh_kernel(
    where_ref,
    att_ref,
    before_ref,
    after_ref,
    query_ref,
    partial_ref,
    stats_ref,
    stream_ref,
    qkv_ref,
    out_w_ref,
    up_ref,
    down_ref,
    gain_ref,
    final_ref,
    side_ref,
    attended_ref,
):
    nodes, width = stream_ref.shape
    head = width // HEADS
    blocks = nodes // BLK
    scaling = head ** (-0.5)
    has_before = where_ref[0] > 0
    has_after = where_ref[0] < where_ref[1] - 1
    kv = qkv_ref[:, width:]
    side_ref[:nodes, :] = dot(before_ref[...], kv).astype(BF16)
    side_ref[nodes:, :] = dot(after_ref[...], kv).astype(BF16)
    for i in range(blocks):
        rows = slice(i * BLK, (i + 1) * BLK)
        starts = [pl.multiple_of(att_ref[i, k] * BLK, BLK) for k in range(NB)]
        usable = [
            jnp.where(att_ref[i, k] < blocks, has_before, has_after) for k in range(NB)
        ]
        chosen = jnp.concatenate([side_ref[pl.ds(s, BLK), :] for s in starts], axis=0)
        allowed = jnp.concatenate(
            [jnp.full((1, BLK), jnp.where(u, 1.0, 0.0), F32) for u in usable], axis=1
        )
        for h in range(HEADS):
            cols = slice(h * head, (h + 1) * head)
            vcols = slice(width + h * head, width + (h + 1) * head)
            scores = dot_nt(query_ref[rows, cols], chosen[:, cols]) * scaling
            scores = jnp.where(allowed > 0.5, scores, MASKED)
            held = stats_ref[rows, 2 * h : 2 * h + 1]
            highest = jnp.maximum(held, jnp.max(scores, axis=-1, keepdims=True))
            probs = jnp.exp(scores - highest)
            keep = jnp.exp(held - highest)
            totals = stats_ref[rows, 2 * h + 1 : 2 * h + 2] * keep + jnp.sum(
                probs, axis=-1, keepdims=True
            )
            combined = partial_ref[rows, cols] * keep + dot(probs.astype(BF16), chosen[:, vcols])
            attended_ref[rows, cols] = (combined / totals).astype(BF16)
    stream = stream_ref[...] + dot(attended_ref[...], out_w_ref[...])
    normed = layer_norm(stream, gain_ref[1:2, :]).astype(BF16)
    hidden_width = up_ref.shape[1]
    for c in range(0, hidden_width, width):
        hidden = silu(dot(normed, up_ref[:, c : c + width])).astype(BF16)
        stream = stream + dot(hidden, down_ref[c : c + width, :])
    final = layer_norm(stream, gain_ref[2:3, :])
    final_ref[...] = final.T.astype(BF16)


def decode_kernel(peers, cap, got_ref, final_ref, embed_ref, dec1_ref, dec2_ref, out_ref):
    width = got_ref.shape[2]
    nodes = final_ref.shape[1]
    channels = dec2_ref.shape[0]
    step = ROWS // cap
    final = final_ref[...]
    for o in range(0, peers, step):
        rows = got_ref[o : o + step, :cap, :].reshape(ROWS, width)
        latent = silu(dot_nt(embed_ref[...], rows)).astype(BF16)
        places = lax.broadcasted_iota(jnp.int32, (nodes, ROWS), 0).astype(F32)
        mix = jnp.zeros((nodes, ROWS), F32)
        for k in range(3):
            slot = slot_row(got_ref, o, step, cap, k, 3)
            weight = weight_row(got_ref, o, step, cap, 6 + k)
            mix = mix + jnp.where(places == slot, weight, 0.0)
        upper = mix.astype(BF16)
        lower = (mix - upper.astype(F32)).astype(BF16)
        pulled = (dot(final, upper) + dot(final, lower)).astype(BF16)
        mixed = (latent.astype(F32) + pulled.astype(F32)).astype(BF16)
        decoded = silu(dot(dec1_ref[...], mixed)).astype(BF16)
        result = dot(dec2_ref[...], decoded).astype(BF16)
        for r in range(step):
            out_ref[o + r, :channels, :] = result[:, r * cap : (r + 1) * cap]
            out_ref[o + r, channels:, :] = jnp.zeros((RET - channels, cap), BF16)


def return_kernel(peers, cap, got_ref, owner_ref, rank_ref, out_ref):
    channels, grid = out_ref.shape
    placed = rank_onehot(rank_ref[...], cap)
    chosen = owner_onehot(owner_ref[...], peers)
    total = jnp.zeros((RET, grid), F32)
    step = 4
    for o in range(0, peers, step):
        spread = dot(got_ref[o : o + step].reshape(step * RET, cap), placed)
        for r in range(step):
            total = total + spread[r * RET : (r + 1) * RET] * chosen[o + r : o + r + 1, :]
    out_ref[...] = total[:channels].astype(BF16)


def body(
    grid_in,
    mesh_state,
    enc_owner,
    enc_slot,
    dec_owner,
    dec_slot,
    dec_weight,
    att_list,
    w_embed,
    w_message,
    norm_gain,
    w_qkv,
    w_out,
    w_up,
    w_down,
    w_dec1,
    w_dec2,
):
    peers = lax.axis_size("band")
    place = lax.axis_index("band")
    grid = grid_in.shape[0]
    nodes, width = mesh_state.shape
    cap = 2 * grid // peers
    channels = w_dec2.shape[1]
    slots = peers * cap

    def exchange(x):
        return lax.all_to_all(x, "band", split_axis=0, concat_axis=0, tiled=True)

    enc_send, _ = bucket(enc_owner.T, enc_slot.T, None, grid_in, peers, cap)
    enc_got = exchange(enc_send)
    dec_send, dec_rank = bucket(dec_owner.T, dec_slot.T, dec_weight.T, grid_in, peers, cap)
    dec_got = exchange(dec_send)

    stream, normed = call(
        functools.partial(encode_kernel, peers, cap),
        (
            jax.ShapeDtypeStruct((nodes, width), F32),
            jax.ShapeDtypeStruct((nodes, width), BF16),
        ),
        (enc_got, mesh_state, w_embed, w_message, norm_gain),
        flops=2 * slots * width * (grid_in.shape[1] + width + nodes),
        moved=2 * slots * grid_in.shape[1] + 8 * nodes * width,
    )
    up = [(i, i + 1) for i in range(peers - 1)]
    down = [(j, i) for i, j in up]
    before = lax.ppermute(normed, "band", up)
    after = lax.ppermute(normed, "band", down)
    query, partial, stats = call(
        local_kernel,
        (
            jax.ShapeDtypeStruct((nodes, width), BF16),
            jax.ShapeDtypeStruct((nodes, width), F32),
            jax.ShapeDtypeStruct((nodes, BLK), F32),
        ),
        (normed, w_qkv[0]),
        flops=2 * nodes * width * (3 * width + 2 * nodes),
        moved=2 * nodes * width * 8,
    )
    where = jnp.stack([place, jnp.int32(peers)]).astype(jnp.int32)
    final = call(
        mesh_kernel,
        jax.ShapeDtypeStruct((width, nodes), BF16),
        (
            where,
            att_list,
            before,
            after,
            query,
            partial,
            stats,
            stream,
            w_qkv[0],
            w_out[0],
            w_up[0],
            w_down[0],
            norm_gain,
        ),
        scratch=(
            pltpu.VMEM((2 * nodes, 2 * width), BF16),
            pltpu.VMEM((nodes, width), BF16),
        ),
        smem=(0, 1),
        flops=2 * nodes * width * (4 * width + 2 * nodes + width + 2 * w_up.shape[2]),
        moved=2 * width * (3 * width + width + 2 * w_up.shape[2]) + 10 * nodes * width,
    )
    result = call(
        functools.partial(decode_kernel, peers, cap),
        jax.ShapeDtypeStruct((peers, RET, cap), BF16),
        (dec_got, final, w_embed.T, w_dec1.T, w_dec2.T),
        flops=2 * slots * width * (grid_in.shape[1] + 2 * nodes + width + 128),
        moved=2 * slots * grid_in.shape[1] + 2 * nodes * width,
    )
    returned = exchange(result)
    return call(
        functools.partial(return_kernel, peers, cap),
        jax.ShapeDtypeStruct((channels, grid), BF16),
        (returned, dec_owner.T, dec_rank),
        flops=2 * peers * RET * cap * grid,
        moved=2 * slots * RET,
    )


def solution(mesh):
    return jax.shard_map(
        body,
        mesh=mesh,
        in_specs=(
            P(("ens", "band"), None),
            P("band", None),
            P("band", None),
            P("band", None),
            P("band", None),
            P("band", None),
            P("band", None),
            P("band", None),
            P(),
            P(),
            P(),
            P(),
            P(),
            P(),
            P(),
            P(),
            P(),
        ),
        out_specs=P(None, ("ens", "band")),
        check_vma=False,
    )
```

time: 314 us -> 123 us (0.39)
  the two profiles are of different devices: /device:TPU:11 before, /device:TPU:0 now
where the time goes in v1:
time: 123 us; the launch traced here: 122 us
  Pallas kernels  36 us (29%)
  blocking collectives  32.6 us (27%)
  waiting for transfers between devices  22.5 us (18%)
  starting transfers between devices  18.9 us (15%)
  local copies, waits for them, and re-layouts  11.7 us (10%)
    pallas_call x7, Pallas kernels, call(): pl.pallas_call(kernel, out_shape=out_shape, in_specs=specs, out_specs=out...  36 us
    all_to_all x1, blocking collectives, exchange(): return lax.all_to_all(x, 'band', split_axis=0, concat_axis=0, tiled=True)  32.6 us
    all_to_all x2, waiting for transfers between devices, exchange(): return lax.all_to_all(x, 'band', split_axis=0, concat_axis=0, tiled=True)  22.5 us
    all_to_all x2, starting transfers between devices, exchange(): return lax.all_to_all(x, 'band', split_axis=0, concat_axis=0, tiled=True)  15.1 us
    unnamed x46, local copies, waits for them, and re-layouts  11.7 us
  transfers between devices with their start and end apart: 4, of which 1 were waited for; matrix products, arithmetic and copies ran while one was open for 1% of the time, Pallas kernels for 20%

profile of v1, /device:TPU:0, one launch (start us, length us, event | category | flops | bytes accessed | tf_op | source)
XLA Modules:
  0.0 122.1 jit_solution(18153268926570842109)
XLA Ops:
  0.0 1.0 copy-done.5
  1.0 0.7 copy-done.14
  1.7 0.7 copy-done.15
  2.4 2.6 %shard_map.164 = (bf16[16,144,256]{2,1,0:T(8,128)(2,1)}, f32[1,1024]{1,0:T(1,128)}) custom-call(s32[1,1024]{1,0:T(1,128)S(1)} %bitcast.23, s32[1,1024]{1,0:T(1,128)S(1)} %bitcast.24, bf16[1024,256]{1,0:T(8,128)(2,1)S(1)} %copy-done.5), custom_call_target="tpu_custom_call" | custom-call | flops 1073741824 | bytes 1703936 | tf_op jit(solution)/shard_map/pallas_call | solution.py:51
  5.0 7.5 %all-to-all-start.1 = ((bf16[16,144,256]{2,1,0:T(8,128)(2,1)}), bf16[16,144,256]{2,1,0:T(8,128)(2,1)S(1)}, u32[]{:S(2)}, u32[]{:S(2)}) async-start(bf16[16,144,256]{2,1,0:T(8,128)(2,1)} %get-tuple-element.14), calls=%async_computation.1 | async-start | bytes 2359296 | tf_op jit(solution)/shard_map/all_to_all | solution.py:322
  12.6 2.6 %shard_map.163 = (bf16[16,144,256]{2,1,0:T(8,128)(2,1)}, f32[1,1024]{1,0:T(1,128)S(1)}) custom-call(s32[1,1024]{1,0:T(1,128)S(1)} %bitcast.25, s32[3,1024]{1,0:T(4,128)S(1)} %bitcast.21, f32[3,1024]{1,0:T(4,128)S(1)} %bitcast.22, bf16[1024,256]{1,0:T(8,128)(2,1)S(1)} %copy-done.6), custom_call_target="tpu_custom_call" | custom-call | flops 1073741824 | bytes 1703936 | tf_op jit(solution)/shard_map/pallas_call | solution.py:51
  15.2 22.5 %all-to-all-done.1.got_ref = bf16[16,144,256]{2,1,0:T(8,128)(2,1)S(1)} async-done(((bf16[16,144,256]{2,1,0:T(8,128)(2,1)}), bf16[16,144,256]{2,1,0:T(8,128)(2,1)S(1)}, u32[]{:S(2)}, u32[]{:S(2)}) %all-to-all-start.1) | async-done | bytes 1179680 | tf_op jit(solution)/shard_map/all_to_all | solution.py:322
  37.7 7.6 %all-to-all-start = ((bf16[16,144,256]{2,1,0:T(8,128)(2,1)}), bf16[16,144,256]{2,1,0:T(8,128)(2,1)S(1)}, u32[]{:S(2)}, u32[]{:S(2)}) async-start(bf16[16,144,256]{2,1,0:T(8,128)(2,1)} %get-tuple-element.13), calls=%async_computation | async-start | bytes 2359296 | tf_op jit(solution)/shard_map/all_to_all | solution.py:322
  45.3 1.0 copy-done.8
  46.4 4.7 %shard_map.165 = (f32[512,512]{1,0:T(8,128)S(1)}, bf16[512,512]{1,0:T(8,128)(2,1)}) custom-call(bf16[16,144,256]{2,1,0:T(8,128)(2,1)S(1)} %all-to-all-done.1.got_ref, bf16[512,512]{1,0:T(8,128)(2,1)S(1)} %copy-done.7, bf16[256,512]{1,0:T(8,128)(2,1)S(1)} %copy-done, bf16[512,512]{1,0:T(8,128)(2,1)S(1)} %copy-done.8, f32[3,512]{1,0:T(4,128)S(1)} %copy-done.13), custom_call_target="tpu_custom_call" | custom-call | flops 2684354560 | bytes 3145728 | tf_op jit(solution)/shard_map/pallas_call | solution.py:51
  51.0 1.0 copy-done.18
  52.0 2.3 %collective-permute-start = (bf16[512,512]{1,0:T(8,128)(2,1)}, bf16[512,512]{1,0:T(8,128)(2,1)S(1)}, u32[]{:S(2)}, u32[]{:S(2)}) collective-permute-start(bf16[512,512]{1,0:T(8,128)(2,1)} %get-tuple-element.15.normed_ref), channel_id=1, source_target_pairs={{0,1},{1,2},{2,3},{3,4},{4,5},{5,6},{6,7},{7,8},{8,9},{9,10},{10,1... | collective-permute-start | bytes 1572872 | tf_op jit(solution)/shard_map/ppermute | solution.py:341
  54.3 1.5 %collective-permute-start.1 = (bf16[512,512]{1,0:T(8,128)(2,1)}, bf16[512,512]{1,0:T(8,128)(2,1)}, u32[]{:S(2)}, u32[]{:S(2)}) collective-permute-start(bf16[512,512]{1,0:T(8,128)(2,1)} %get-tuple-element.15.normed_ref), channel_id=1, source_target_pairs={{1,0},{2,1},{3,2},{4,3},{5,4},{6,5},{7,6},{8,7},{9,8},{10,9},{11,1... | collective-permute-start | bytes 1572872 | tf_op jit(solution)/shard_map/ppermute | solution.py:342
  56.0 1.3 %copy.19 = bf16[512,512]{0,1:T(8,128)(2,1)S(1)} copy(bf16[512,512]{1,0:T(8,128)(2,1)} %param.32) | data formatting | bytes 1048576 | tf_op args[15]
  57.3 1.4 %copy-done.3 = bf16[1,512,1536]{2,1,0:T(8,128)(2,1)S(1)} copy-done((bf16[1,512,1536]{2,1,0:T(8,128)(2,1)S(1)}, bf16[1,512,1536]{2,1,0:T(8,128)(2,1)}, u32[]{:S(2)}) %copy-start.3) | copy-done | bytes 1572888
  58.7 3.8 %shard_map.166 = (bf16[512,512]{1,0:T(8,128)(2,1)S(1)}, f32[512,512]{1,0:T(8,128)S(1)}, f32[512,128]{1,0:T(8,128)S(1)}) custom-call(bf16[512,512]{1,0:T(8,128)(2,1)} %get-tuple-element.15.normed_ref, bf16[512,1536]{1,0:T(8,128)(2,1)S(1)} %bitcast.17), custom_call_target="tpu_custom_call" | custom-call | flops 1342177280 | bytes 4194304 | tf_op jit(solution)/shard_map/pallas_call | solution.py:51
  62.6 1.4 %copy-done.4 = bf16[1,512,1536]{2,1,0:T(8,128)(2,1)S(1)} copy-done((bf16[1,512,1536]{2,1,0:T(8,128)(2,1)S(1)}, bf16[1,512,1536]{2,1,0:T(8,128)(2,1)}, u32[]{:S(2)}) %copy-start.4) | copy-done | bytes 1572888
  64.0 1.2 %copy-done.19 = f32[512,512]{1,0:T(8,128)S(1)} copy-done((f32[512,512]{1,0:T(8,128)S(1)}, f32[512,512]{1,0:T(8,128)}, u32[]{:S(2)}) %copy-start.19) | copy-done | bytes 1048600
  65.2 13.3 %shard_map.167.final_ref = bf16[512,512]{1,0:T(8,128)(2,1)S(1)} custom-call(s32[2]{0:T(128)S(1)} %pad_add_fusion.where_ref, s32[4,4]{1,0:T(4,128)S(1)} %copy-done.17, bf16[512,512]{1,0:T(8,128)(2,1)S(1)} %collective-permute-done.before_ref, bf16[512,512]{1,0:T(8,128)(2,1)} %collective-permute-done.1.after_ref, ...), custom_call_target="tpu_custom_call" | custom-call | flops 4026531840 | bytes 8912896 | tf_op jit(solution)/shard_map/pallas_call | solution.py:51
  78.5 0.8 copy-done.20
  79.3 1.0 copy-done.21
  80.3 7.5 %shard_map.168 = bf16[16,96,128]{2,1,0:T(8,128)(2,1)S(1)} custom-call(bf16[16,144,256]{2,1,0:T(8,128)(2,1)S(1)} %all-to-all-done.got_ref, bf16[512,512]{1,0:T(8,128)(2,1)S(1)} %copy-done.21, bf16[512,256]{1,0:T(8,128)(2,1)S(1)} %bitcast.14, bf16[512,512]{1,0:T(8,128)(2,1)S(1)} %bitcast.13, bf16[84,512]{1,0:T(8,128)(2,1)S(1)} %bitcast.20), custom_call_target="tpu_custom_call" | custom-call | flops 4026531840 | bytes 1572864 | tf_op jit(solution)/shard_map/pallas_call | solution.py:51
  87.9 32.6 %all_to_all.15.got_ref = bf16[16,96,128]{2,1,0:T(8,128)(2,1)S(1)} all-to-all(bf16[16,96,128]{2,1,0:T(8,128)(2,1)S(1)} %shard_map.168), channel_id=1, replica_groups=mesh['ens'=2,'band'=16] {'band'}, dimensions={0} | all-to-all | bytes 786432 | tf_op jit(solution)/shard_map/all_to_all | solution.py:322
  120.5 1.6 %shard_map.169 = bf16[84,1024]{1,0:T(8,128)(2,1)} custom-call(bf16[16,96,128]{2,1,0:T(8,128)(2,1)S(1)} %all_to_all.15.got_ref, s32[1,1024]{1,0:T(1,128)S(1)} %bitcast.26, f32[1,1024]{1,0:T(1,128)S(1)} %get-tuple-element.20.rank_ref), custom_call_target="tpu_custom_call" | custom-call | flops 402653184 | bytes 393216 | tf_op jit(solution)/shard_map/pallas_call | solution.py:51
  (39 shorter events, 0.3 us)
Async XLA Ops:
  0.0 1.0 copy-start.5
  5.0 7.5 %copy-start.6 = (bf16[1024,256]{1,0:T(8,128)(2,1)S(1)}, bf16[1024,256]{1,0:T(8,128)(2,1)}, u32[]{:S(2)}) copy-start(bf16[1024,256]{1,0:T(8,128)(2,1)} %refs_2_.1) | copy-start | bytes 1572868
  5.0 7.5 %copy-start.11 = (s32[1024,3]{0,1:T(4,128)S(1)}, s32[1024,3]{0,1:T(4,128)}, u32[]{:S(2)}) copy-start(s32[1024,3]{0,1:T(4,128)} %param.22) | copy-start | bytes 36868
  5.0 7.5 %copy-start.12 = (f32[1024,3]{0,1:T(4,128)S(1)}, f32[1024,3]{0,1:T(4,128)}, u32[]{:S(2)}) copy-start(f32[1024,3]{0,1:T(4,128)} %param.23) | copy-start | bytes 36868
  5.0 7.5 %copy-start.16 = (s32[1024,1]{0,1:T(1,128)S(1)}, s32[1024,1]{0,1:T(1,128)}, u32[]{:S(2)}) copy-start(s32[1024,1]{0,1:T(1,128)} %param.21) | copy-start | bytes 12292
  5.0 32.6 %all-to-all-start.1 = ((bf16[16,144,256]{2,1,0:T(8,128)(2,1)}), bf16[16,144,256]{2,1,0:T(8,128)(2,1)S(1)}, u32[]{:S(2)}, u32[]{:S(2)}) async-start(bf16[16,144,256]{2,1,0:T(8,128)(2,1)} %get-tuple-element.14), calls=%async_computation.1 | async-start | bytes 2359296 | tf_op jit(solution)/shard_map/all_to_all | solution.py:322
  37.7 7.6 %copy-start = (bf16[256,512]{1,0:T(8,128)(2,1)S(1)}, bf16[256,512]{1,0:T(8,128)(2,1)}, u32[]{:S(2)}) copy-start(bf16[256,512]{1,0:T(8,128)(2,1)} %embed_ref.1) | copy-start | bytes 786436
  37.7 7.6 %copy-start.7 = (bf16[512,512]{1,0:T(8,128)(2,1)S(1)}, bf16[512,512]{1,0:T(8,128)(2,1)}, u32[]{:S(2)}) copy-start(bf16[512,512]{1,0:T(8,128)(2,1)} %state_ref.1) | copy-start | bytes 1572868
  37.7 7.6 %copy-start.13 = (f32[3,512]{1,0:T(4,128)S(1)}, f32[3,512]{1,0:T(4,128)}, u32[]{:S(2)}) copy-start(f32[3,512]{1,0:T(4,128)} %gain_ref.3) | copy-start | bytes 18436
  37.7 41.6 %all-to-all-start = ((bf16[16,144,256]{2,1,0:T(8,128)(2,1)}), bf16[16,144,256]{2,1,0:T(8,128)(2,1)S(1)}, u32[]{:S(2)}, u32[]{:S(2)}) async-start(bf16[16,144,256]{2,1,0:T(8,128)(2,1)} %get-tuple-element.13), calls=%async_computation | async-start | bytes 2359296 | tf_op jit(solution)/shard_map/all_to_all | solution.py:322
  45.3 1.0 copy-start.8
  51.0 1.0 copy-start.18
  52.0 10.5 %collective-permute-start = (bf16[512,512]{1,0:T(8,128)(2,1)}, bf16[512,512]{1,0:T(8,128)(2,1)S(1)}, u32[]{:S(2)}, u32[]{:S(2)}) collective-permute-start(bf16[512,512]{1,0:T(8,128)(2,1)} %get-tuple-element.15.normed_ref), channel_id=1, source_target_pairs={{0,1},{1,2},{2,3},{3,4},{4,5},{5,6},{6,7},{7,8},{8,9},{9,10},{10,1... | collective-permute-start | bytes 1572872 | tf_op jit(solution)/shard_map/ppermute | solution.py:341
  54.3 8.2 %collective-permute-start.1 = (bf16[512,512]{1,0:T(8,128)(2,1)}, bf16[512,512]{1,0:T(8,128)(2,1)}, u32[]{:S(2)}, u32[]{:S(2)}) collective-permute-start(bf16[512,512]{1,0:T(8,128)(2,1)} %get-tuple-element.15.normed_ref), channel_id=1, source_target_pairs={{1,0},{2,1},{3,2},{4,3},{5,4},{6,5},{7,6},{8,7},{9,8},{10,9},{11,1... | collective-permute-start | bytes 1572872 | tf_op jit(solution)/shard_map/ppermute | solution.py:342
  57.3 1.4 %copy-start.3 = (bf16[1,512,1536]{2,1,0:T(8,128)(2,1)S(1)}, bf16[1,512,1536]{2,1,0:T(8,128)(2,1)}, u32[]{:S(2)}) copy-start(bf16[1,512,1536]{2,1,0:T(8,128)(2,1)} %param.28) | copy-start | bytes 4718596
  58.7 3.8 %copy-start.1 = (bf16[1,512,2048]{2,1,0:T(8,128)(2,1)S(1)}, bf16[1,512,2048]{2,1,0:T(8,128)(2,1)}, u32[]{:S(2)}) copy-start(bf16[1,512,2048]{2,1,0:T(8,128)(2,1)} %param.30) | copy-start | bytes 6291460
  58.7 3.8 %copy-start.2 = (bf16[1,2048,512]{2,1,0:T(8,128)(2,1)S(1)}, bf16[1,2048,512]{2,1,0:T(8,128)(2,1)}, u32[]{:S(2)}) copy-start(bf16[1,2048,512]{2,1,0:T(8,128)(2,1)} %param.31) | copy-start | bytes 6291460
  58.7 3.8 %copy-start.9 = (bf16[1,512,512]{2,1,0:T(8,128)(2,1)S(1)}, bf16[1,512,512]{2,1,0:T(8,128)(2,1)}, u32[]{:S(2)}) copy-start(bf16[1,512,512]{2,1,0:T(8,128)(2,1)} %param.29) | copy-start | bytes 1572868
  58.7 3.8 %copy-start.17 = (s32[4,4]{1,0:T(4,128)S(1)}, s32[4,4]{1,0:T(4,128)}, u32[]{:S(2)}) copy-start(s32[4,4]{1,0:T(4,128)} %att_ref.1) | copy-start | bytes 196
  62.5 1.4 %copy-start.4 = (bf16[1,512,1536]{2,1,0:T(8,128)(2,1)S(1)}, bf16[1,512,1536]{2,1,0:T(8,128)(2,1)}, u32[]{:S(2)}) copy-start(bf16[1,512,1536]{2,1,0:T(8,128)(2,1)} %param.28) | copy-start | bytes 4718596
  64.0 1.2 %copy-start.19 = (f32[512,512]{1,0:T(8,128)S(1)}, f32[512,512]{1,0:T(8,128)}, u32[]{:S(2)}) copy-start(f32[512,512]{1,0:T(8,128)} %copy-done.18) | copy-start | bytes 3145732
  65.2 14.1 %copy-start.10 = (bf16[512,84]{0,1:T(8,128)(2,1)S(1)}, bf16[512,84]{0,1:T(8,128)(2,1)}, u32[]{:S(2)}) copy-start(bf16[512,84]{0,1:T(8,128)(2,1)} %param.33) | copy-start | bytes 258052
  78.5 0.8 copy-start.20
  79.3 1.0 copy-start.21
  (2 other events, 1.4 us)

commit v2 on v1

v2 whole, which is shorter than its diff:
```python
import functools

import jax
import jax.numpy as jnp
from jax import lax
from jax.experimental import pallas as pl
from jax.experimental.pallas import tpu as pltpu
from jax.sharding import PartitionSpec as P

HEADS = 4
BLK = 128
NB = 4
META = 16
ROWS = 512
LOW = 32
MASKED = -1e30
LOG2E = 1.4426950408889634
VMEM_LIMIT = 24 * 1024 * 1024

epsilon = 1e-05

F32 = jnp.float32
BF16 = jnp.bfloat16


def dot(a, b):
    return jnp.dot(a, b, preferred_element_type=F32)


def dot_nt(a, b):
    return lax.dot_general(a, b, (((1,), (1,)), ((), ())), preferred_element_type=F32)


def silu(v):
    half = 0.5 * v
    return half + half * jnp.tanh(half)


def layer_norm(values, gains):
    average = jnp.mean(values, axis=-1, keepdims=True)
    centred = values - average
    spread_sq = jnp.mean(centred * centred, axis=-1, keepdims=True)
    return centred * lax.rsqrt(spread_sq + epsilon) * gains


class Held:
    def __init__(self, far, near, sem):
        self.near = near
        self.copy = pltpu.make_async_copy(far, near, sem)
        self.state = 0

    def start(self):
        if self.state == 0:
            self.copy.start()
            self.state = 1

    def __call__(self):
        self.start()
        if self.state == 1:
            self.copy.wait()
            self.state = 2
        return self.near


class Sent:
    def __init__(self, near, far, sem):
        self.near = near
        self.copy = pltpu.make_async_copy(near, far, sem)
        self.started = False

    def send(self):
        if not self.started:
            self.copy.start()
            self.started = True


def call(kernel, outs, args, kinds, scratch=(), late=(), flops=0, moved=0):
    n_in, n_out = len(args), len(outs)
    far_in = [i for i in range(n_in) if kinds[i] == "H"]
    far_out = [i for i in range(n_out) if outs[i][2] == "H"]

    def wrapped(*refs):
        ins, results = list(refs[:n_in]), list(refs[n_in : n_in + n_out])
        rest = list(refs[n_in + n_out :])
        sems = rest.pop(0)
        for n, i in enumerate(far_in):
            ins[i] = Held(ins[i], rest.pop(0), sems.at[n])
            if i not in late:
                ins[i].start()
        for n, i in enumerate(far_out):
            results[i] = Sent(rest.pop(0), results[i], sems.at[len(far_in) + n])
        kernel(*ins, *results, *rest)
        for i in far_out:
            results[i].send()
        for i in far_in:
            ins[i]()
        for i in far_out:
            results[i].copy.wait()

    spaces = {"V": pltpu.VMEM, "H": pltpu.HBM, "S": pltpu.SMEM}

    def spec(kind):
        return pl.BlockSpec(memory_space=pl.ANY if kind == "H" else spaces[kind])

    def placed(x, kind):
        return x if kind == "S" else pltpu.with_memory_space_constraint(x, spaces[kind])

    return pl.pallas_call(
        wrapped,
        out_shape=tuple(
            pltpu.HBM(shape, dtype) if kind == "H" else jax.ShapeDtypeStruct(shape, dtype)
            for shape, dtype, kind in outs
        ),
        in_specs=[spec(kind) for kind in kinds],
        out_specs=tuple(spec(kind) for _, _, kind in outs),
        scratch_shapes=[pltpu.SemaphoreType.DMA((max(1, len(far_in) + len(far_out)),))]
        + [pltpu.VMEM(args[i].shape, args[i].dtype) for i in far_in]
        + [pltpu.VMEM(outs[i][0], outs[i][1]) for i in far_out]
        + list(scratch),
        compiler_params=pltpu.CompilerParams(vmem_limit_bytes=VMEM_LIMIT),
        cost_estimate=pl.CostEstimate(flops=flops, bytes_accessed=moved, transcendentals=0),
    )(*[placed(x, kind) for x, kind in zip(args, kinds)])


def owner_onehot(owner, peers):
    places = lax.broadcasted_iota(jnp.int32, (peers, owner.shape[1]), 0)
    return jnp.where(places == owner, 1.0, 0.0).astype(F32)


def rank_onehot(rank, cap):
    places = lax.broadcasted_iota(jnp.int32, (cap, rank.shape[1]), 0).astype(F32)
    return jnp.where(places == rank, 1.0, 0.0).astype(BF16)


def bucket_kernel(peers, cap, weighted, turned, *refs):
    refs = list(refs)
    held_owner, held_slot = refs.pop(0), refs.pop(0)
    held_weight = refs.pop(0) if weighted else None
    held_rows = refs.pop(0)
    turns = [refs.pop(0) for _ in range(turned)]
    out, rank_out = refs.pop(0), refs.pop(0) if weighted else None
    turned_outs = [refs.pop(0) for _ in range(turned)]
    send_ref = out.near
    grid, width = held_rows.near.shape
    part = 256 if grid % 256 == 0 else grid
    upto = jnp.where(
        lax.broadcasted_iota(jnp.int32, (part, part), 0)
        <= lax.broadcasted_iota(jnp.int32, (part, part), 1),
        1.0,
        0.0,
    ).astype(BF16)
    owner = held_owner()[...]
    chosen = owner_onehot(owner, peers)
    chosen16 = chosen.astype(BF16)
    carry = jnp.zeros((peers, 1), F32)
    ranks = []
    for c in range(grid // part):
        span = slice(c * part, (c + 1) * part)
        counts = dot(chosen16[:, span], upto) + carry
        carry = counts[:, part - 1 :]
        ranks.append(jnp.sum(chosen[:, span] * counts, axis=0, keepdims=True) - 1.0)
    rank = jnp.concatenate(ranks, axis=1)
    if weighted:
        rank_out.near[...] = rank
    placed = rank_onehot(rank, cap)

    slots = held_slot()[...]
    pieces = [(slots // LOW).astype(F32), (slots % LOW).astype(F32)]
    if weighted:
        pieces.append(held_weight()[...])
    used = sum(p.shape[0] for p in pieces)
    pieces.append(jnp.zeros((META - used, grid), F32))
    features = jnp.concatenate(pieces, axis=0).astype(BF16).astype(F32)
    spread = (chosen[:, None, :] * features[None, :, :]).reshape(peers * META, grid)
    meta = dot_nt(spread.astype(BF16), placed).reshape(peers, META, cap)
    send_ref[:, cap:, :] = jnp.zeros((peers, META, width), BF16)
    send_ref[:, cap:, :cap] = meta.astype(BF16)

    rows = held_rows()[...]
    step = ROWS // cap
    for o in range(0, peers, step):
        select = (chosen16[o : o + step, None, :] * placed[None, :, :]).reshape(step * cap, grid)
        moved = dot(select, rows)
        send_ref[o : o + step, :cap, :] = moved.astype(BF16).reshape(step, cap, width)
    out.send()
    for f, t in zip(turns, turned_outs):
        t.near[...] = f()[...].T


def bucket(owner, slots, weights, rows, turns, peers, cap):
    grid, width = rows.shape
    weighted = weights is not None
    args = (owner, slots) + ((weights,) if weighted else ()) + (rows,) + turns
    outs = [((peers, cap + META, width), BF16, "H")]
    if weighted:
        outs.append(((1, grid), F32, "H"))
    outs += [(x.shape[::-1], x.dtype, "H") for x in turns]
    return call(
        functools.partial(bucket_kernel, peers, cap, weighted, len(turns)),
        outs,
        args,
        "H" * len(args),
        flops=2 * peers * cap * grid * width,
        moved=2 * (grid * width + peers * (cap + META) * width),
    )


def meta_row(got_ref, o, step, cap, row):
    return jnp.concatenate(
        [got_ref[r, cap:, :cap].astype(F32)[row : row + 1, :] for r in range(o, o + step)],
        axis=1,
    )


def slot_row(got_ref, o, step, cap, low, count):
    return meta_row(got_ref, o, step, cap, low) * LOW + meta_row(
        got_ref, o, step, cap, low + count
    )


def encode_kernel(peers, cap, got_ref, embed, message_w, state, gain, stream, normed, target_ref):
    width = got_ref.shape[2]
    nodes = stream.near.shape[0]
    step = ROWS // cap
    places = lax.broadcasted_iota(jnp.int32, (nodes, ROWS), 0).astype(F32)
    for n, o in enumerate(range(0, peers, step)):
        slot = slot_row(got_ref, o, step, cap, 0, 1)
        target_ref[n] = jnp.where(places == slot, 1.0, 0.0).astype(BF16)
    total = None
    for n, o in enumerate(range(0, peers, step)):
        rows = got_ref[o : o + step, :cap, :].reshape(ROWS, width)
        latent = silu(dot(rows, embed()[...])).astype(BF16)
        message = dot(latent, message_w()[...]).astype(BF16)
        arrived = dot(target_ref[n], message)
        total = state()[...].astype(F32) + arrived if total is None else total + arrived
    normed.near[...] = layer_norm(total, gain()[0:1, :]).astype(BF16)
    normed.send()
    stream.near[...] = total


def local_kernel(normed, qkv, query, partial, stats):
    nodes, width = query.near.shape
    head = width // HEADS
    rate = head ** (-0.5) * LOG2E
    held = normed()[...]
    qkv_ref = qkv()
    queries = dot(held, qkv_ref[:, :width]).astype(BF16)
    query.near[...] = queries
    query.send()
    key = dot(held, qkv_ref[:, width : 2 * width]).astype(BF16)
    value = dot(held, qkv_ref[:, 2 * width :]).astype(BF16)
    ones = jnp.ones((nodes, BLK), BF16)
    lanes = lax.broadcasted_iota(jnp.int32, (nodes, BLK), 1)
    packed = jnp.zeros((nodes, BLK), F32)
    for h in range(HEADS):
        cols = slice(h * head, (h + 1) * head)
        scores = dot_nt(queries[:, cols], key[:, cols])
        highest = jnp.max(scores, axis=-1, keepdims=True)
        weights = jnp.exp2((scores - highest) * rate).astype(BF16)
        sums = dot(weights, jnp.concatenate([value[:, cols], ones], axis=1))
        partial.near[:, cols] = sums[:, :head]
        packed = jnp.where(lanes == h, highest, packed)
        packed = jnp.where(lanes == HEADS + h, sums[:, head:], packed)
    stats.near[...] = packed


def tail_kernel(
    peers,
    cap,
    where_ref,
    att_ref,
    before_ref,
    after_ref,
    got_ref,
    qkv,
    query,
    stats,
    partial,
    stream_in,
    out_w,
    up_w,
    down_w,
    gain,
    embed,
    dec1,
    dec2,
    out_ref,
    key_ref,
    value_ref,
    attended_ref,
    mix_ref,
):
    nodes, width = attended_ref.shape
    head = width // HEADS
    blocks = nodes // BLK
    rate = head ** (-0.5) * LOG2E
    has_before = where_ref[0] > 0
    has_after = where_ref[0] < where_ref[1] - 1
    step = ROWS // cap
    columns = got_ref.shape[2]

    places = lax.broadcasted_iota(jnp.int32, (nodes, ROWS), 0).astype(F32)
    for n, o in enumerate(range(0, peers, step)):
        mix = jnp.zeros((nodes, ROWS), F32)
        for k in range(3):
            slot = slot_row(got_ref, o, step, cap, k, 3)
            weight = meta_row(got_ref, o, step, cap, 6 + k)
            mix = mix + jnp.where(places == slot, weight, 0.0)
        mix_ref[n] = mix.astype(BF16)

    qkv_ref = qkv()
    for n, side in enumerate((before_ref, after_ref)):
        rows = slice(n * nodes, (n + 1) * nodes)
        key_ref[rows, :] = dot(side[...], qkv_ref[:, width : 2 * width]).astype(BF16)
        value = dot(side[...], qkv_ref[:, 2 * width :]).astype(BF16)
        for h in range(HEADS):
            value_ref[rows, 2 * h * head : (2 * h + 1) * head] = value[:, h * head : (h + 1) * head]
    for h in range(HEADS):
        value_ref[:, (2 * h + 1) * head : (2 * h + 2) * head] = jnp.ones((2 * nodes, head), BF16)

    query_ref, stats_ref, partial_ref = query(), stats(), partial()
    starts, allowed = [], []
    for i in range(blocks):
        starts.append([pl.multiple_of(att_ref[i, k] * BLK, BLK) for k in range(NB)])
        usable = [
            jnp.where(att_ref[i, k] < blocks, has_before, has_after) for k in range(NB)
        ]
        row = jnp.concatenate(
            [jnp.full((1, BLK), jnp.where(u, 0.0, MASKED), F32) for u in usable], axis=1
        )
        allowed.append(row)

    def chosen(ref, i, span):
        return jnp.concatenate([ref[pl.ds(s, BLK), span] for s in starts[i]], axis=0)

    for h in range(HEADS):
        cols = slice(h * head, (h + 1) * head)
        both = slice(2 * h * head, (2 * h + 2) * head)
        scores = jnp.concatenate(
            [
                dot_nt(query_ref[i * BLK : (i + 1) * BLK, cols], chosen(key_ref, i, cols))
                + allowed[i]
                for i in range(blocks)
            ],
            axis=0,
        )
        held = stats_ref[:, h : h + 1]
        highest = jnp.maximum(held, jnp.max(scores, axis=-1, keepdims=True))
        weights = jnp.exp2((scores - highest) * rate).astype(BF16)
        keep = jnp.exp2((held - highest) * rate)
        sums = jnp.concatenate(
            [
                dot(weights[i * BLK : (i + 1) * BLK], chosen(value_ref, i, both))
                for i in range(blocks)
            ],
            axis=0,
        )
        totals = stats_ref[:, HEADS + h : HEADS + h + 1] * keep + sums[:, head:]
        combined = partial_ref[:, cols] * keep + sums[:, :head]
        attended_ref[:, cols] = (combined / totals).astype(BF16)

    stream = stream_in()[...] + dot(attended_ref[...], out_w()[...])
    normed = layer_norm(stream, gain()[1:2, :]).astype(BF16)
    up_ref, down_ref = up_w(), down_w()
    hidden_width = up_ref.shape[1]
    for c in range(0, hidden_width, width):
        hidden = silu(dot(normed, up_ref[:, c : c + width])).astype(BF16)
        stream = stream + dot(hidden, down_ref[c : c + width, :])
    final = layer_norm(stream, gain()[2:3, :]).astype(BF16).T

    embed_ref, dec1_ref, dec2_ref = embed(), dec1(), dec2()
    for n, o in enumerate(range(0, peers, step)):
        rows = got_ref[o : o + step, :cap, :].reshape(ROWS, columns)
        latent = silu(dot_nt(embed_ref[...], rows)).astype(BF16)
        pulled = dot(final, mix_ref[n]).astype(BF16)
        mixed = (latent.astype(F32) + pulled.astype(F32)).astype(BF16)
        decoded = silu(dot(dec1_ref[...], mixed)).astype(BF16)
        result = dot(dec2_ref[...], decoded).astype(BF16)
        for r in range(step):
            out_ref[o + r] = result[:, r * cap : (r + 1) * cap]


TAIL_KINDS = "SSVVVHHHHHHHHHHHH"


def tail_scratch(nodes, width, slots):
    return (
        pltpu.VMEM((2 * nodes, width), BF16),
        pltpu.VMEM((2 * nodes, 2 * width), BF16),
        pltpu.VMEM((nodes, width), BF16),
        pltpu.VMEM((slots // ROWS, nodes, ROWS), BF16),
    )


def return_kernel(peers, cap, got_ref, rank, owner, out_ref):
    channels, grid = out_ref.shape
    placed = rank_onehot(rank[...], cap)
    chosen = owner_onehot(owner[...], peers)
    total = jnp.zeros((channels, grid), F32)
    for o in range(peers):
        total = total + dot(got_ref[o], placed) * chosen[o : o + 1, :]
    out_ref[...] = total.astype(BF16)


def body(
    grid_in,
    mesh_state,
    enc_owner,
    enc_slot,
    dec_owner,
    dec_slot,
    dec_weight,
    att_list,
    w_embed,
    w_message,
    norm_gain,
    w_qkv,
    w_out,
    w_up,
    w_down,
    w_dec1,
    w_dec2,
):
    peers = lax.axis_size("band")
    place = lax.axis_index("band")
    grid = grid_in.shape[0]
    nodes, width = mesh_state.shape
    cap = 2 * grid // peers
    channels = w_dec2.shape[1]
    slots = peers * cap

    def exchange(x):
        return lax.all_to_all(x, "band", split_axis=0, concat_axis=0, tiled=True)

    (enc_send,) = bucket(enc_owner.T, enc_slot.T, None, grid_in, (), peers, cap)
    enc_got = exchange(enc_send)
    dec_send, rank, embed_t, dec1_t = bucket(
        dec_owner.T, dec_slot.T, dec_weight.T, grid_in, (w_embed, w_dec1), peers, cap
    )
    dec_got = exchange(dec_send)

    stream, normed = call(
        functools.partial(encode_kernel, peers, cap),
        (((nodes, width), F32, "H"), ((nodes, width), BF16, "H")),
        (enc_got, w_embed, w_message, mesh_state, norm_gain),
        "VHHHH",
        scratch=(pltpu.VMEM((slots // ROWS, nodes, ROWS), BF16),),
        flops=2 * slots * width * (grid_in.shape[1] + width + nodes),
        moved=2 * slots * grid_in.shape[1] + 8 * nodes * width,
    )
    up = [(i, i + 1) for i in range(peers - 1)]
    down = [(j, i) for i, j in up]
    before = lax.ppermute(normed, "band", up)
    after = lax.ppermute(normed, "band", down)
    query, partial, stats = call(
        local_kernel,
        (((nodes, width), BF16, "H"), ((nodes, width), F32, "H"), ((nodes, BLK), F32, "H")),
        (normed, w_qkv[0]),
        "HH",
        flops=2 * nodes * width * (3 * width + 2 * nodes),
        moved=2 * nodes * width * 8,
    )
    where = jnp.stack([place, jnp.int32(peers)]).astype(jnp.int32)
    (result,) = call(
        functools.partial(tail_kernel, peers, cap),
        (((peers, channels, cap), BF16, "V"),),
        (
            where,
            att_list,
            before,
            after,
            dec_got,
            w_qkv[0],
            query,
            stats,
            partial,
            stream,
            w_out[0],
            w_up[0],
            w_down[0],
            norm_gain,
            embed_t,
            dec1_t,
            w_dec2.T,
        ),
        TAIL_KINDS,
        scratch=tail_scratch(nodes, width, slots),
        flops=2 * nodes * width * (4 * width + 2 * nodes + width + 2 * w_up.shape[2])
        + 2 * slots * width * (grid_in.shape[1] + nodes + width + 128),
        moved=2 * width * (3 * width + width + 2 * w_up.shape[2]) + 10 * nodes * width,
    )
    returned = exchange(result)
    (denoised,) = call(
        functools.partial(return_kernel, peers, cap),
        (((channels, grid), BF16, "V"),),
        (returned, rank, dec_owner.T),
        "VVV",
        flops=2 * slots * channels * grid,
        moved=2 * slots * channels,
    )
    return denoised


def solution(mesh):
    return jax.shard_map(
        body,
        mesh=mesh,
        in_specs=(
            P(("ens", "band"), None),
            P("band", None),
            P("band", None),
            P("band", None),
            P("band", None),
            P("band", None),
            P("band", None),
            P("band", None),
            P(),
            P(),
            P(),
            P(),
            P(),
            P(),
            P(),
            P(),
            P(),
        ),
        out_specs=P(None, ("ens", "band")),
        check_vma=False,
    )
```

time: 123 us -> 112 us (0.911)
  local copies, waits for them, and re-layouts: 11.7 us -> 0.02 us
  blocking collectives: 32.6 us -> 24.2 us
  waiting for transfers between devices: 22.5 us -> 30.6 us
  Pallas kernels: 36 us -> 37.9 us
    unnamed x46 -> x6, local copies, waits for them, and re-layouts: 11.7 us -> 0.02 us
    all_to_all x1, blocking collectives: 32.6 us -> 24.2 us  [exchange(): return lax.all_to_all(x, 'band', split_axis=0, concat_axis=0, tiled=True)]
    all_to_all x2, waiting for transfers between devices: 22.5 us -> 30.6 us  [exchange(): return lax.all_to_all(x, 'band', split_axis=0, concat_axis=0, tiled=True)]
    pallas_call x7 -> x6, Pallas kernels: 36 us -> 37.9 us  [call(): pl.pallas_call(wrapped, out_shape=tuple((pltpu.HBM(shape, dtype) if kind...]
  transfers between devices with their start and end apart: 4 -> 4, of which waited for: 1 -> 2; matrix products, arithmetic and copies ran while one was open for 1% -> 0% of each run, Pallas kernels for 20% -> 14%
where the time goes in v2:
time: 112 us
  Pallas kernels  37.9 us (34%)
  waiting for transfers between devices  30.6 us (27%)
  blocking collectives  24.2 us (22%)
  starting transfers between devices  18.7 us (17%)
    pallas_call x6, Pallas kernels, call(): pl.pallas_call(wrapped, out_shape=tuple((pltpu.HBM(shape, dtype) if kind...  37.9 us
    all_to_all x2, waiting for transfers between devices, exchange(): return lax.all_to_all(x, 'band', split_axis=0, concat_axis=0, tiled=True)  30.6 us
    all_to_all x1, blocking collectives, exchange(): return lax.all_to_all(x, 'band', split_axis=0, concat_axis=0, tiled=True)  24.2 us
    all_to_all x2, starting transfers between devices, exchange(): return lax.all_to_all(x, 'band', split_axis=0, concat_axis=0, tiled=True)  14.9 us
    ppermute x1, starting transfers between devices, body(): before = lax.ppermute(normed, 'band', up)  2.33 us
  transfers between devices with their start and end apart: 4, of which 2 were waited for; matrix products, arithmetic and copies ran while one was open for 0% of the time, Pallas kernels for 14%

profile of v2, /device:TPU:0, one launch (start us, length us, event | category | flops | bytes accessed | tf_op | source)
XLA Modules:
  0.0 111.7 jit_solution(9413685745676721950)
XLA Ops:
  0.0 3.9 %shard_map.163 = bf16[16,144,256]{2,1,0:T(8,128)(2,1)} custom-call(s32[1,1024]{1,0:T(1,128)} %bitcast.21, s32[1,1024]{1,0:T(1,128)} %bitcast.22, bf16[1024,256]{1,0:T(8,128)(2,1)} %refs_3_.3), custom_call_target="tpu_custom_call" | custom-call | flops 1073741824 | bytes 1703936 | tf_op jit(solution)/shard_map/pallas_call | solution.py:108
  3.9 7.4 %all-to-all-start = ((bf16[16,144,256]{2,1,0:T(8,128)(2,1)}), bf16[16,144,256]{2,1,0:T(8,128)(2,1)S(1)}, u32[]{:S(2)}, u32[]{:S(2)}) async-start(bf16[16,144,256]{2,1,0:T(8,128)(2,1)} %shard_map.163), calls=%async_computation | async-start | bytes 2359296 | tf_op jit(solution)/shard_map/all_to_all | solution.py:433
  11.3 4.3 %shard_map.165 = (bf16[16,144,256]{2,1,0:T(8,128)(2,1)}, f32[1,1024]{1,0:T(1,128)}, bf16[512,256]{1,0:T(8,128)(2,1)}, bf16[512,512]{1,0:T(8,128)(2,1)}) custom-call(s32[1,1024]{1,0:T(1,128)} %bitcast.11, s32[3,1024]{1,0:T(4,128)} %bitcast.19, f32[3,1024]{1,0:T(4,128)} %bitcast.20, bf16[1024,256]{1,0:T(8,128)(2,1)} %refs_3_.3, bf16[256,512]{1,0:T(8,128)(2,1)} %refs_4_.3, ...), custom_call_target="tpu_custom_call" | custom-call | flops 1073741824 | bytes 1703936 | tf_op jit(solution)/shard_map/pallas_call | solution.py:108
  15.6 20.9 %all-to-all-done.refs_0_ = bf16[16,144,256]{2,1,0:T(8,128)(2,1)S(1)} async-done(((bf16[16,144,256]{2,1,0:T(8,128)(2,1)}), bf16[16,144,256]{2,1,0:T(8,128)(2,1)S(1)}, u32[]{:S(2)}, u32[]{:S(2)}) %all-to-all-start) | async-done | bytes 1179680 | tf_op jit(solution)/shard_map/all_to_all | solution.py:433
  36.5 7.5 %all-to-all-start.1 = ((bf16[16,144,256]{2,1,0:T(8,128)(2,1)}), bf16[16,144,256]{2,1,0:T(8,128)(2,1)S(1)}, u32[]{:S(2)}, u32[]{:S(2)}) async-start(bf16[16,144,256]{2,1,0:T(8,128)(2,1)} %get-tuple-element.15), calls=%async_computation.1 | async-start | bytes 2359296 | tf_op jit(solution)/shard_map/all_to_all | solution.py:433
  43.9 6.3 %shard_map.164 = (f32[512,512]{1,0:T(8,128)}, bf16[512,512]{1,0:T(8,128)(2,1)}) custom-call(bf16[16,144,256]{2,1,0:T(8,128)(2,1)S(1)} %all-to-all-done.refs_0_, bf16[256,512]{1,0:T(8,128)(2,1)} %refs_4_.3, bf16[512,512]{1,0:T(8,128)(2,1)} %refs_2_.3, bf16[512,512]{1,0:T(8,128)(2,1)} %refs_3_.2, f32[3,512]{1,0:T(4,128)} %refs_13_.1), custom_call_target="tpu_custom_call" | custom-call | flops 2684354560 | bytes 3145728 | tf_op jit(solution)/shard_map/pallas_call | solution.py:108
  50.2 2.3 %collective-permute-start = (bf16[512,512]{1,0:T(8,128)(2,1)}, bf16[512,512]{1,0:T(8,128)(2,1)S(1)}, u32[]{:S(2)}, u32[]{:S(2)}) collective-permute-start(bf16[512,512]{1,0:T(8,128)(2,1)} %get-tuple-element.14.refs_0_), channel_id=1, source_target_pairs={{0,1},{1,2},{2,3},{3,4},{4,5},{5,6},{6,7},{7,8},{8,9},{9,10},{10,1... | collective-permute-start | bytes 1572872 | tf_op jit(solution)/shard_map/ppermute | solution.py:453
  52.6 1.5 %collective-permute-start.1 = (bf16[512,512]{1,0:T(8,128)(2,1)}, bf16[512,512]{1,0:T(8,128)(2,1)S(1)}, u32[]{:S(2)}, u32[]{:S(2)}) collective-permute-start(bf16[512,512]{1,0:T(8,128)(2,1)} %get-tuple-element.14.refs_0_), channel_id=1, source_target_pairs={{1,0},{2,1},{3,2},{4,3},{5,4},{6,5},{7,6},{8,7},{9,8},{10,9},{11,1... | collective-permute-start | bytes 1572872 | tf_op jit(solution)/shard_map/ppermute | solution.py:454
  54.0 0.1 pad_add_fusion.refs_0_
  54.1 0.0 copy-start.1
  54.1 5.2 %shard_map.166 = (bf16[512,512]{1,0:T(8,128)(2,1)}, f32[512,512]{1,0:T(8,128)}, f32[512,128]{1,0:T(8,128)}) custom-call(bf16[512,512]{1,0:T(8,128)(2,1)} %get-tuple-element.14.refs_0_, bf16[512,1536]{1,0:T(8,128)(2,1)} %bitcast.15), custom_call_target="tpu_custom_call" | custom-call | flops 1342177280 | bytes 4194304 | tf_op jit(solution)/shard_map/pallas_call | solution.py:108
  59.3 9.8 %all-to-all-done.1.refs_4_ = bf16[16,144,256]{2,1,0:T(8,128)(2,1)S(1)} async-done(((bf16[16,144,256]{2,1,0:T(8,128)(2,1)}), bf16[16,144,256]{2,1,0:T(8,128)(2,1)S(1)}, u32[]{:S(2)}, u32[]{:S(2)}) %all-to-all-start.1) | async-done | bytes 1179680 | tf_op jit(solution)/shard_map/all_to_all | solution.py:433
  69.1 0.0 collective-permute-done.refs_2_
  69.1 0.0 collective-permute-done.1.refs_3_
  69.1 0.0 copy-done.1
  69.1 0.0 copy-start
  69.1 0.0 copy-start.2
  69.1 16.6 %shard_map.167 = bf16[16,84,128]{2,1,0:T(8,128)(2,1)S(1)} custom-call(s32[2]{0:T(128)S(1)} %pad_add_fusion.refs_0_, s32[4,4]{1,0:T(4,128)S(1)} %copy-done.1, bf16[512,512]{1,0:T(8,128)(2,1)S(1)} %collective-permute-done.refs_2_, bf16[512,512]{1,0:T(8,128)(2,1)S(1)} %collective-permute-done.1.refs_3_, bf16[16,144,256]{2,1,0:T(8,128)(2,1)S(1)} %all-to-all-done.1.refs_4_, ...), custom_call_target="tpu_custom_call" | custom-call | flops 6979321856 | bytes 8912896 | tf_op jit(solution)/shard_map/pallas_call | solution.py:108
  85.7 24.2 %all_to_all.15.refs_0_ = bf16[16,84,128]{2,1,0:T(8,128)(2,1)S(1)} all-to-all(bf16[16,84,128]{2,1,0:T(8,128)(2,1)S(1)} %shard_map.167), channel_id=1, replica_groups=mesh['ens'=2,'band'=16] {'band'}, dimensions={0} | all-to-all | bytes 688128 | tf_op jit(solution)/shard_map/all_to_all | solution.py:433
  109.9 0.0 copy-done
  109.9 0.0 copy-done.2
  109.9 1.7 %shard_map.168 = bf16[84,1024]{1,0:T(8,128)(2,1)} custom-call(bf16[16,84,128]{2,1,0:T(8,128)(2,1)S(1)} %all_to_all.15.refs_0_, f32[1,1024]{1,0:T(1,128)S(1)} %copy-done.2, s32[1,1024]{1,0:T(1,128)S(1)} %bitcast.12), custom_call_target="tpu_custom_call" | custom-call | flops 352321536 | bytes 344064 | tf_op jit(solution)/shard_map/pallas_call | solution.py:108
Async XLA Ops:
  3.9 32.5 %all-to-all-start = ((bf16[16,144,256]{2,1,0:T(8,128)(2,1)}), bf16[16,144,256]{2,1,0:T(8,128)(2,1)S(1)}, u32[]{:S(2)}, u32[]{:S(2)}) async-start(bf16[16,144,256]{2,1,0:T(8,128)(2,1)} %shard_map.163), calls=%async_computation | async-start | bytes 2359296 | tf_op jit(solution)/shard_map/all_to_all | solution.py:433
  36.5 32.6 %all-to-all-start.1 = ((bf16[16,144,256]{2,1,0:T(8,128)(2,1)}), bf16[16,144,256]{2,1,0:T(8,128)(2,1)S(1)}, u32[]{:S(2)}, u32[]{:S(2)}) async-start(bf16[16,144,256]{2,1,0:T(8,128)(2,1)} %get-tuple-element.15), calls=%async_computation.1 | async-start | bytes 2359296 | tf_op jit(solution)/shard_map/all_to_all | solution.py:433
  50.2 18.9 %collective-permute-start = (bf16[512,512]{1,0:T(8,128)(2,1)}, bf16[512,512]{1,0:T(8,128)(2,1)S(1)}, u32[]{:S(2)}, u32[]{:S(2)}) collective-permute-start(bf16[512,512]{1,0:T(8,128)(2,1)} %get-tuple-element.14.refs_0_), channel_id=1, source_target_pairs={{0,1},{1,2},{2,3},{3,4},{4,5},{5,6},{6,7},{7,8},{8,9},{9,10},{10,1... | collective-permute-start | bytes 1572872 | tf_op jit(solution)/shard_map/ppermute | solution.py:453
  52.6 16.5 %collective-permute-start.1 = (bf16[512,512]{1,0:T(8,128)(2,1)}, bf16[512,512]{1,0:T(8,128)(2,1)S(1)}, u32[]{:S(2)}, u32[]{:S(2)}) collective-permute-start(bf16[512,512]{1,0:T(8,128)(2,1)} %get-tuple-element.14.refs_0_), channel_id=1, source_target_pairs={{1,0},{2,1},{3,2},{4,3},{5,4},{6,5},{7,6},{8,7},{9,8},{10,9},{11,1... | collective-permute-start | bytes 1572872 | tf_op jit(solution)/shard_map/ppermute | solution.py:454
  54.1 15.0 %copy-start.1 = (s32[4,4]{1,0:T(4,128)S(1)}, s32[4,4]{1,0:T(4,128)}, u32[]{:S(2)}) copy-start(s32[4,4]{1,0:T(4,128)} %refs_1_.3) | copy-start | bytes 196
  69.1 40.8 %copy-start = (s32[1024,1]{0,1:T(1,128)S(1)}, s32[1024,1]{0,1:T(1,128)}, u32[]{:S(2)}) copy-start(s32[1024,1]{0,1:T(1,128)} %param.21) | copy-start | bytes 12292
  69.1 40.8 %copy-start.2 = (f32[1,1024]{1,0:T(1,128)S(1)}, f32[1,1024]{1,0:T(1,128)}, u32[]{:S(2)}) copy-start(f32[1,1024]{1,0:T(1,128)} %get-tuple-element.22.refs_1_) | copy-start | bytes 12292

commit v3 on v2

--- a/solution.py
+++ b/solution.py
@@ -184,17 +184,20 @@
         send_ref[o : o + step, :cap, :] = moved.astype(BF16).reshape(step, cap, width)
     out.send()
     for f, t in zip(turns, turned_outs):
-        t.near[...] = f()[...].T
+        source = f()
+        skipped = source.shape[1] - t.near.shape[0]
+        t.near[...] = source[:, skipped:].T
+        t.send()
 
 
 def bucket(owner, slots, weights, rows, turns, peers, cap):
     grid, width = rows.shape
     weighted = weights is not None
-    args = (owner, slots) + ((weights,) if weighted else ()) + (rows,) + turns
+    args = (owner, slots) + ((weights,) if weighted else ()) + (rows,) + tuple(x for x, _ in turns)
     outs = [((peers, cap + META, width), BF16, "H")]
     if weighted:
         outs.append(((1, grid), F32, "H"))
-    outs += [(x.shape[::-1], x.dtype, "H") for x in turns]
+    outs += [((count, x.shape[0]), x.dtype, "H") for x, count in turns]
     return call(
         functools.partial(bucket_kernel, peers, cap, weighted, len(turns)),
         outs,
@@ -218,50 +221,58 @@
     )
 
 
-def encode_kernel(peers, cap, got_ref, embed, message_w, state, gain, stream, normed, target_ref):
+def encode_kernel(peers, cap, got_ref, embed, message_w, state, gain, stream, normed, target_ref, message_ref):
     width = got_ref.shape[2]
     nodes = stream.near.shape[0]
     step = ROWS // cap
     places = lax.broadcasted_iota(jnp.int32, (nodes, ROWS), 0).astype(F32)
-    for n, o in enumerate(range(0, peers, step)):
+    starts = range(0, peers, step)
+    for n, o in enumerate(starts):
         slot = slot_row(got_ref, o, step, cap, 0, 1)
-        target_ref[n] = jnp.where(places == slot, 1.0, 0.0).astype(BF16)
-    total = None
-    for n, o in enumerate(range(0, peers, step)):
-        rows = got_ref[o : o + step, :cap, :].reshape(ROWS, width)
-        latent = silu(dot(rows, embed()[...])).astype(BF16)
-        message = dot(latent, message_w()[...]).astype(BF16)
-        arrived = dot(target_ref[n], message)
-        total = state()[...].astype(F32) + arrived if total is None else total + arrived
+        target_ref[:, n * ROWS : (n + 1) * ROWS] = jnp.where(places == slot, 1.0, 0.0).astype(BF16)
+    embed_ref = embed()
+    latents = [
+        silu(dot(got_ref[o : o + step, :cap, :].reshape(ROWS, width), embed_ref[...])).astype(BF16)
+        for o in starts
+    ]
+    message_w_ref = message_w()
+    for n, latent in enumerate(latents):
+        message_ref[n * ROWS : (n + 1) * ROWS, :] = dot(latent, message_w_ref[...]).astype(BF16)
+    total = state()[...].astype(F32) + dot(target_ref[...], message_ref[...])
     normed.near[...] = layer_norm(total, gain()[0:1, :]).astype(BF16)
     normed.send()
     stream.near[...] = total
 
 
-def local_kernel(normed, qkv, query, partial, stats):
-    nodes, width = query.near.shape
+def layer_norm_columns(values, gains):
+    average = jnp.mean(values, axis=0, keepdims=True)
+    centred = values - average
+    spread_sq = jnp.mean(centred * centred, axis=0, keepdims=True)
+    return centred * lax.rsqrt(spread_sq + epsilon) * gains
+
+
+def local_kernel(normed, qkv, value_t, stream, query_t, partial_t, stats, stream_t):
+    width, nodes = query_t.near.shape
     head = width // HEADS
     rate = head ** (-0.5) * LOG2E
     held = normed()[...]
     qkv_ref = qkv()
-    queries = dot(held, qkv_ref[:, :width]).astype(BF16)
-    query.near[...] = queries
-    query.send()
+    queries = dot(held, qkv_ref[:, :width]).astype(BF16).T
+    query_t.near[...] = queries
+    query_t.send()
     key = dot(held, qkv_ref[:, width : 2 * width]).astype(BF16)
-    value = dot(held, qkv_ref[:, 2 * width :]).astype(BF16)
-    ones = jnp.ones((nodes, BLK), BF16)
-    lanes = lax.broadcasted_iota(jnp.int32, (nodes, BLK), 1)
-    packed = jnp.zeros((nodes, BLK), F32)
+    value = dot_nt(value_t()[...], held).astype(BF16)
     for h in range(HEADS):
-        cols = slice(h * head, (h + 1) * head)
-        scores = dot_nt(queries[:, cols], key[:, cols])
-        highest = jnp.max(scores, axis=-1, keepdims=True)
-        weights = jnp.exp2((scores - highest) * rate).astype(BF16)
-        sums = dot(weights, jnp.concatenate([value[:, cols], ones], axis=1))
-        partial.near[:, cols] = sums[:, :head]
-        packed = jnp.where(lanes == h, highest, packed)
-        packed = jnp.where(lanes == HEADS + h, sums[:, head:], packed)
-    stats.near[...] = packed
+        rows = slice(h * head, (h + 1) * head)
+        scores = dot(key[:, rows], queries[rows, :])
+        highest = jnp.max(scores, axis=0, keepdims=True)
+        probs = jnp.exp2((scores - highest) * rate)
+        stats.near[h : h + 1, :] = highest
+        stats.near[HEADS + h : HEADS + h + 1, :] = jnp.sum(probs, axis=0, keepdims=True)
+        partial_t.near[rows, :] = dot(value[rows, :], probs.astype(BF16))
+    stats.send()
+    partial_t.send()
+    stream_t.near[...] = stream()[...].T
 
 
 def tail_kernel(
@@ -273,24 +284,26 @@
     after_ref,
     got_ref,
     qkv,
-    query,
+    value_t,
+    query_t,
     stats,
-    partial,
-    stream_in,
-    out_w,
-    up_w,
-    down_w,
-    gain,
-    embed,
-    dec1,
-    dec2,
+    partial_t,
+    stream_t,
+    out_t,
+    up_t,
+    down_t,
+    gain_t,
+    embed_t,
+    dec1_t,
+    dec2_t,
     out_ref,
     key_ref,
     value_ref,
     attended_ref,
     mix_ref,
+    hidden_ref,
 ):
-    nodes, width = attended_ref.shape
+    width, nodes = attended_ref.shape
     head = width // HEADS
     blocks = nodes // BLK
     rate = head ** (-0.5) * LOG2E
@@ -298,9 +311,10 @@
     has_after = where_ref[0] < where_ref[1] - 1
     step = ROWS // cap
     columns = got_ref.shape[2]
+    chunks = list(enumerate(range(0, peers, step)))
 
     places = lax.broadcasted_iota(jnp.int32, (nodes, ROWS), 0).astype(F32)
-    for n, o in enumerate(range(0, peers, step)):
+    for n, o in chunks:
         mix = jnp.zeros((nodes, ROWS), F32)
         for k in range(3):
             slot = slot_row(got_ref, o, step, cap, k, 3)
@@ -308,87 +322,87 @@
             mix = mix + jnp.where(places == slot, weight, 0.0)
         mix_ref[n] = mix.astype(BF16)
 
-    qkv_ref = qkv()
+    qkv_ref, value_t_ref = qkv(), value_t()
     for n, side in enumerate((before_ref, after_ref)):
-        rows = slice(n * nodes, (n + 1) * nodes)
-        key_ref[rows, :] = dot(side[...], qkv_ref[:, width : 2 * width]).astype(BF16)
-        value = dot(side[...], qkv_ref[:, 2 * width :]).astype(BF16)
-        for h in range(HEADS):
-            value_ref[rows, 2 * h * head : (2 * h + 1) * head] = value[:, h * head : (h + 1) * head]
+        key_ref[n * nodes : (n + 1) * nodes, :] = dot(
+            side[...], qkv_ref[:, width : 2 * width]
+        ).astype(BF16)
+        value = dot_nt(value_t_ref[...], side[...]).astype(BF16)
+        for i in range(blocks):
+            value_ref[n * blocks + i] = value[:, i * BLK : (i + 1) * BLK]
+
+    query_ref, stats_ref, partial_ref = query_t(), stats(), partial_t()
+    named = [[att_ref[i, k] for k in range(NB)] for i in range(blocks)]
+    starts = [[pl.multiple_of(w * BLK, BLK) for w in row] for row in named]
+    allowed = [
+        [jnp.where(jnp.where(w < blocks, has_before, has_after), 0.0, MASKED) for w in row]
+        for row in named
+    ]
     for h in range(HEADS):
-        value_ref[:, (2 * h + 1) * head : (2 * h + 2) * head] = jnp.ones((2 * nodes, head), BF16)
-
-    query_ref, stats_ref, partial_ref = query(), stats(), partial()
-    starts, allowed = [], []
-    for i in range(blocks):
-        starts.append([pl.multiple_of(att_ref[i, k] * BLK, BLK) for k in range(NB)])
-        usable = [
-            jnp.where(att_ref[i, k] < blocks, has_before, has_after) for k in range(NB)
-        ]
-        row = jnp.concatenate(
-            [jnp.full((1, BLK), jnp.where(u, 0.0, MASKED), F32) for u in usable], axis=1
+        rows = slice(h * head, (h + 1) * head)
+        scores = []
+        for i in range(blocks):
+            queries = query_ref[rows, i * BLK : (i + 1) * BLK]
+            keys = jnp.concatenate([key_ref[pl.ds(s, BLK), rows] for s in starts[i]], axis=0)
+            found = dot(keys, queries)
+            scores.append(
+                jnp.concatenate(
+                    [found[k * BLK : (k + 1) * BLK] + allowed[i][k] for k in range(NB)], axis=0
+                )
+            )
+        scores = jnp.concatenate(scores, axis=1)
+        held = stats_ref[h : h + 1, :]
+        highest = jnp.maximum(held, jnp.max(scores, axis=0, keepdims=True))
+        probs = jnp.exp2((scores - highest) * rate)
+        keep = jnp.exp2((held - highest) * rate)
+        totals = stats_ref[HEADS + h : HEADS + h + 1, :] * keep + jnp.sum(
+            probs, axis=0, keepdims=True
         )
-        allowed.append(row)
-
-    def chosen(ref, i, span):
-        return jnp.concatenate([ref[pl.ds(s, BLK), span] for s in starts[i]], axis=0)
-
-    for h in range(HEADS):
-        cols = slice(h * head, (h + 1) * head)
-        both = slice(2 * h * head, (2 * h + 2) * head)
-        scores = jnp.concatenate(
-            [
-                dot_nt(query_ref[i * BLK : (i + 1) * BLK, cols], chosen(key_ref, i, cols))
-                + allowed[i]
-                for i in range(blocks)
-            ],
-            axis=0,
+        weights = probs.astype(BF16)
+        remote = []
+        for i in range(blocks):
+            values = jnp.concatenate([value_ref[w, rows, :] for w in named[i]], axis=1)
+            remote.append(dot(values, weights[:, i * BLK : (i + 1) * BLK]))
+        combined = partial_ref[rows, :] * keep + jnp.concatenate(remote, axis=1)
+        attended_ref[rows, :] = (combined / totals).astype(BF16)
+
+    gains = gain_t()[...]
+    stream = stream_t()[...] + dot(out_t()[...], attended_ref[...])
+    normed = layer_norm_columns(stream, gains[:, 1:2]).astype(BF16)
+    up_ref = up_t()
+    for c in range(0, up_ref.shape[0], width):
+        hidden_ref[c : c + width, :] = silu(dot(up_ref[c : c + width, :], normed)).astype(BF16)
+    stream = stream + dot(down_t()[...], hidden_ref[...])
+    final = layer_norm_columns(stream, gains[:, 2:3]).astype(BF16)
+
+    embed_ref, dec1_ref, dec2_ref = embed_t(), dec1_t(), dec2_t()
+    latents = [
+        silu(dot_nt(embed_ref[...], got_ref[o : o + step, :cap, :].reshape(ROWS, columns))).astype(
+            BF16
         )
-        held = stats_ref[:, h : h + 1]
-        highest = jnp.maximum(held, jnp.max(scores, axis=-1, keepdims=True))
-        weights = jnp.exp2((scores - highest) * rate).astype(BF16)
-        keep = jnp.exp2((held - highest) * rate)
-        sums = jnp.concatenate(
-            [
-                dot(weights[i * BLK : (i + 1) * BLK], chosen(value_ref, i, both))
-                for i in range(blocks)
-            ],
-            axis=0,
-        )
-        totals = stats_ref[:, HEADS + h : HEADS + h + 1] * keep + sums[:, head:]
-        combined = partial_ref[:, cols] * keep + sums[:, :head]
-        attended_ref[:, cols] = (combined / totals).astype(BF16)
-
-    stream = stream_in()[...] + dot(attended_ref[...], out_w()[...])
-    normed = layer_norm(stream, gain()[1:2, :]).astype(BF16)
-    up_ref, down_ref = up_w(), down_w()
-    hidden_width = up_ref.shape[1]
-    for c in range(0, hidden_width, width):
-        hidden = silu(dot(normed, up_ref[:, c : c + width])).astype(BF16)
-        stream = stream + dot(hidden, down_ref[c : c + width, :])
-    final = layer_norm(stream, gain()[2:3, :]).astype(BF16).T
-
-    embed_ref, dec1_ref, dec2_ref = embed(), dec1(), dec2()
-    for n, o in enumerate(range(0, peers, step)):
-        rows = got_ref[o : o + step, :cap, :].reshape(ROWS, columns)
-        latent = silu(dot_nt(embed_ref[...], rows)).astype(BF16)
-        pulled = dot(final, mix_ref[n]).astype(BF16)
-        mixed = (latent.astype(F32) + pulled.astype(F32)).astype(BF16)
-        decoded = silu(dot(dec1_ref[...], mixed)).astype(BF16)
-        result = dot(dec2_ref[...], decoded).astype(BF16)
+        for _, o in chunks
+    ]
+    pulled = [dot(final, mix_ref[n]).astype(BF16) for n, _ in chunks]
+    mixed = [
+        (latents[n].astype(F32) + pulled[n].astype(F32)).astype(BF16) for n, _ in chunks
+    ]
+    decoded = [silu(dot(dec1_ref[...], mixed[n])).astype(BF16) for n, _ in chunks]
+    for n, o in chunks:
+        result = dot(dec2_ref[...], decoded[n]).astype(BF16)
         for r in range(step):
             out_ref[o + r] = result[:, r * cap : (r + 1) * cap]
 
 
-TAIL_KINDS = "SSVVVHHHHHHHHHHHH"
-
-
-def tail_scratch(nodes, width, slots):
+TAIL_KINDS = "SSVVVHHHHHHHHHHHHH"
+
+
+def tail_scratch(nodes, width, slots, hidden):
     return (
         pltpu.VMEM((2 * nodes, width), BF16),
-        pltpu.VMEM((2 * nodes, 2 * width), BF16),
-        pltpu.VMEM((nodes, width), BF16),
+        pltpu.VMEM((2 * nodes // BLK, width, BLK), BF16),
+        pltpu.VMEM((width, nodes), BF16),
         pltpu.VMEM((slots // ROWS, nodes, ROWS), BF16),
+        pltpu.VMEM((hidden, nodes), BF16),
     )
 
 
@@ -434,8 +448,21 @@
 
     (enc_send,) = bucket(enc_owner.T, enc_slot.T, None, grid_in, (), peers, cap)
     enc_got = exchange(enc_send)
-    dec_send, rank, embed_t, dec1_t = bucket(
-        dec_owner.T, dec_slot.T, dec_weight.T, grid_in, (w_embed, w_dec1), peers, cap
+    dec_send, rank, embed_t, dec1_t, value_t, out_t, up_t, down_t = bucket(
+        dec_owner.T,
+        dec_slot.T,
+        dec_weight.T,
+        grid_in,
+        (
+            (w_embed, width),
+            (w_dec1, width),
+            (w_qkv[0], width),
+            (w_out[0], width),
+            (w_up[0], w_up.shape[2]),
+            (w_down[0], width),
+        ),
+        peers,
+        cap,
     )
     dec_got = exchange(dec_send)
 
@@ -444,7 +471,7 @@
         (((nodes, width), F32, "H"), ((nodes, width), BF16, "H")),
         (enc_got, w_embed, w_message, mesh_state, norm_gain),
         "VHHHH",
-        scratch=(pltpu.VMEM((slots // ROWS, nodes, ROWS), BF16),),
+        scratch=(pltpu.VMEM((nodes, slots), BF16), pltpu.VMEM((slots, width), BF16)),
         flops=2 * slots * width * (grid_in.shape[1] + width + nodes),
         moved=2 * slots * grid_in.shape[1] + 8 * nodes * width,
     )
@@ -452,11 +479,16 @@
     down = [(j, i) for i, j in up]
     before = lax.ppermute(normed, "band", up)
     after = lax.ppermute(normed, "band", down)
-    query, partial, stats = call(
+    query_t, partial_t, stats, stream_t = call(
         local_kernel,
-        (((nodes, width), BF16, "H"), ((nodes, width), F32, "H"), ((nodes, BLK), F32, "H")),
-        (normed, w_qkv[0]),
-        "HH",
+        (
+            ((width, nodes), BF16, "H"),
+            ((width, nodes), F32, "H"),
+            ((2 * HEADS, nodes), F32, "H"),
+            ((width, nodes), F32, "H"),
+        ),
+        (normed, w_qkv[0], value_t, stream),
+        "HHHH",
         flops=2 * nodes * width * (3 * width + 2 * nodes),
         moved=2 * nodes * width * 8,
     )
@@ -471,20 +503,21 @@
             after,
             dec_got,
             w_qkv[0],
-            query,
+            value_t,
+            query_t,
             stats,
-            partial,
-            stream,
-            w_out[0],
-            w_up[0],
-            w_down[0],
-            norm_gain,
+            partial_t,
+            stream_t,
+            out_t,
+            up_t,
+            down_t,
+            norm_gain.T,
             embed_t,
             dec1_t,
             w_dec2.T,
         ),
         TAIL_KINDS,
-        scratch=tail_scratch(nodes, width, slots),
+        scratch=tail_scratch(nodes, width, slots, w_up.shape[2]),
         flops=2 * nodes * width * (4 * width + 2 * nodes + width + 2 * w_up.shape[2])
         + 2 * slots * width * (grid_in.shape[1] + nodes + width + 128),
         moved=2 * width * (3 * width + width + 2 * w_up.shape[2]) + 10 * nodes * width,

time: 112 us -> 110 us (0.982)
  waiting for transfers between devices: 30.6 us -> 26.7 us
    all_to_all x2, waiting for transfers between devices: 30.6 us -> 26.7 us  [exchange(): return lax.all_to_all(x, 'band', split_axis=0, concat_axis=0, tiled=True)]
  transfers between devices with their start and end apart: 4 -> 4, of which waited for: 2 -> 2; matrix products, arithmetic and copies ran while one was open for 0% -> 1% of each run, Pallas kernels for 14% -> 17%
where the time goes in v3:
time: 110 us; the launch traced here: 109 us
  Pallas kernels  38.5 us (35%)
  waiting for transfers between devices  26.7 us (24%)
  blocking collectives  24.2 us (22%)
  starting transfers between devices  18.7 us (17%)
    pallas_call x6, Pallas kernels, call(): pl.pallas_call(wrapped, out_shape=tuple((pltpu.HBM(shape, dtype) if kind...  38.5 us
    all_to_all x2, waiting for transfers between devices, exchange(): return lax.all_to_all(x, 'band', split_axis=0, concat_axis=0, tiled=True)  26.7 us
    all_to_all x1, blocking collectives, exchange(): return lax.all_to_all(x, 'band', split_axis=0, concat_axis=0, tiled=True)  24.2 us
    all_to_all x2, starting transfers between devices, exchange(): return lax.all_to_all(x, 'band', split_axis=0, concat_axis=0, tiled=True)  14.9 us
    ppermute x1, starting transfers between devices, body(): before = lax.ppermute(normed, 'band', up)  2.34 us
  transfers between devices with their start and end apart: 4, of which 2 were waited for; matrix products, arithmetic and copies ran while one was open for 1% of the time, Pallas kernels for 17%

profile of v3, /device:TPU:0, one launch (start us, length us, event | category | flops | bytes accessed | tf_op | source)
XLA Modules:
  0.0 109.3 jit_solution(8691635244549781116)
XLA Ops:
  0.0 4.0 %shard_map.163 = bf16[16,144,256]{2,1,0:T(8,128)(2,1)} custom-call(s32[1,1024]{1,0:T(1,128)} %bitcast.24, s32[1,1024]{1,0:T(1,128)} %bitcast.25, bf16[1024,256]{1,0:T(8,128)(2,1)} %refs_3_.3), custom_call_target="tpu_custom_call" | custom-call | flops 1073741824 | bytes 1703936 | tf_op jit(solution)/shard_map/pallas_call | solution.py:108
  4.0 7.4 %all-to-all-start = ((bf16[16,144,256]{2,1,0:T(8,128)(2,1)}), bf16[16,144,256]{2,1,0:T(8,128)(2,1)S(1)}, u32[]{:S(2)}, u32[]{:S(2)}) async-start(bf16[16,144,256]{2,1,0:T(8,128)(2,1)} %shard_map.163), calls=%async_computation | async-start | bytes 2359296 | tf_op jit(solution)/shard_map/all_to_all | solution.py:447
  11.3 6.3 %shard_map.165 = (bf16[16,144,256]{2,1,0:T(8,128)(2,1)}, f32[1,1024]{1,0:T(1,128)}, bf16[512,256]{1,0:T(8,128)(2,1)}, bf16[512,512]{1,0:T(8,128)(2,1)}, bf16[512...) custom-call(s32[1,1024]{1,0:T(1,128)} %bitcast.12, ...), custom_call_target="tpu_custom_call" | custom-call | flops 1073741824 | bytes 1703936 | tf_op jit(solution)/shard_map/pallas_call | solution.py:108
  17.7 18.8 %all-to-all-done.refs_0_ = bf16[16,144,256]{2,1,0:T(8,128)(2,1)S(1)} async-done(((bf16[16,144,256]{2,1,0:T(8,128)(2,1)}), bf16[16,144,256]{2,1,0:T(8,128)(2,1)S(1)}, u32[]{:S(2)}, u32[]{:S(2)}) %all-to-all-start) | async-done | bytes 1179680 | tf_op jit(solution)/shard_map/all_to_all | solution.py:447
  36.5 7.5 %all-to-all-start.1 = ((bf16[16,144,256]{2,1,0:T(8,128)(2,1)}), bf16[16,144,256]{2,1,0:T(8,128)(2,1)S(1)}, u32[]{:S(2)}, u32[]{:S(2)}) async-start(bf16[16,144,256]{2,1,0:T(8,128)(2,1)} %get-tuple-element.20), calls=%async_computation.1 | async-start | bytes 2359296 | tf_op jit(solution)/shard_map/all_to_all | solution.py:447
  44.0 0.0 copy-start.3
  44.0 6.2 %shard_map.164 = (f32[512,512]{1,0:T(8,128)}, bf16[512,512]{1,0:T(8,128)(2,1)}) custom-call(bf16[16,144,256]{2,1,0:T(8,128)(2,1)S(1)} %all-to-all-done.refs_0_, bf16[256,512]{1,0:T(8,128)(2,1)} %refs_4_.3, bf16[512,512]{1,0:T(8,128)(2,1)} %refs_2_.3, bf16[512,512]{1,0:T(8,128)(2,1)} %refs_3_.2, f32[3,512]{1,0:T(4,128)} %refs_4_.2), custom_call_target="tpu_custom_call" | custom-call | flops 2684354560 | bytes 3145728 | tf_op jit(solution)/shard_map/pallas_call | solution.py:108
  50.2 2.3 %collective-permute-start = (bf16[512,512]{1,0:T(8,128)(2,1)}, bf16[512,512]{1,0:T(8,128)(2,1)S(1)}, u32[]{:S(2)}, u32[]{:S(2)}) collective-permute-start(bf16[512,512]{1,0:T(8,128)(2,1)} %get-tuple-element.19.refs_0_), channel_id=1, source_target_pairs={{0,1},{1,2},{2,3},{3,4},{4,5},{5,6},{6,7},{7,8},{8,9},{9,10},{10,1... | collective-permute-start | bytes 1572872 | tf_op jit(solution)/shard_map/ppermute | solution.py:480
  52.5 1.5 %collective-permute-start.1 = (bf16[512,512]{1,0:T(8,128)(2,1)}, bf16[512,512]{1,0:T(8,128)(2,1)S(1)}, u32[]{:S(2)}, u32[]{:S(2)}) collective-permute-start(bf16[512,512]{1,0:T(8,128)(2,1)} %get-tuple-element.19.refs_0_), channel_id=1, source_target_pairs={{1,0},{2,1},{3,2},{4,3},{5,4},{6,5},{7,6},{8,7},{9,8},{10,9},{11,1... | collective-permute-start | bytes 1572872 | tf_op jit(solution)/shard_map/ppermute | solution.py:481
  54.0 0.0 copy-done.3
  54.0 0.9 copy.18
  54.9 0.1 pad_add_fusion.refs_0_
  54.9 6.3 %shard_map.166 = (bf16[512,512]{1,0:T(8,128)(2,1)}, f32[512,512]{1,0:T(8,128)}, f32[8,512]{1,0:T(8,128)}, f32[512,512]{1,0:T(8,128)}) custom-call(bf16[512,512]{1,0:T(8,128)(2,1)} %get-tuple-element.19.refs_0_, bf16[512,1536]{1,0:T(8,128)(2,1)} %bitcast.17, bf16[512,512]{1,0:T(8,128)(2,1)} %get-tuple-element.21.refs_2_.refs_6_, ...), custom_call_target="tpu_custom_call" | custom-call | flops 1342177280 | bytes 4194304 | tf_op jit(solution)/shard_map/pallas_call | solution.py:108
  61.2 7.9 %all-to-all-done.1.refs_4_ = bf16[16,144,256]{2,1,0:T(8,128)(2,1)S(1)} async-done(((bf16[16,144,256]{2,1,0:T(8,128)(2,1)}), bf16[16,144,256]{2,1,0:T(8,128)(2,1)S(1)}, u32[]{:S(2)}, u32[]{:S(2)}) %all-to-all-start.1) | async-done | bytes 1179680 | tf_op jit(solution)/shard_map/all_to_all | solution.py:447
  69.1 0.0 collective-permute-done.refs_2_
  69.1 0.0 collective-permute-done.1.refs_3_
  69.1 0.0 copy-done.2
  69.1 0.0 copy-start
  69.1 0.0 copy-start.1
  69.1 14.1 %shard_map.167 = bf16[16,84,128]{2,1,0:T(8,128)(2,1)S(1)} custom-call(s32[2]{0:T(128)S(1)} %pad_add_fusion.refs_0_, s32[4,4]{1,0:T(4,128)S(1)} %copy-done.2, bf16[512,512]{1,0:T(8,128)(2,1)S(1)} %collective-permute-done.refs_2_, bf16[512,512]{1,0:T(8,128)(2,1)S(1)} %collective-permute-done.1.refs_3_, bf16[16,144,256]{2,1,0:T(8,128)(2,1)S(1)} %all-to-all-done.1.refs_4_, ...), custom_call_target="tpu_custom_call" | custom-call | flops 6979321856 | bytes 8912896 | tf_op jit(solution)/shard_map/pallas_call | solution.py:108
  83.3 24.2 %all_to_all.15.refs_0_ = bf16[16,84,128]{2,1,0:T(8,128)(2,1)S(1)} all-to-all(bf16[16,84,128]{2,1,0:T(8,128)(2,1)S(1)} %shard_map.167), channel_id=1, replica_groups=mesh['ens'=2,'band'=16] {'band'}, dimensions={0} | all-to-all | bytes 688128 | tf_op jit(solution)/shard_map/all_to_all | solution.py:447
  107.4 0.0 copy-done
  107.5 0.0 copy-done.1
  107.5 1.7 %shard_map.168 = bf16[84,1024]{1,0:T(8,128)(2,1)} custom-call(bf16[16,84,128]{2,1,0:T(8,128)(2,1)S(1)} %all_to_all.15.refs_0_, f32[1,1024]{1,0:T(1,128)S(1)} %copy-done.1, s32[1,1024]{1,0:T(1,128)S(1)} %bitcast.13), custom_call_target="tpu_custom_call" | custom-call | flops 352321536 | bytes 344064 | tf_op jit(solution)/shard_map/pallas_call | solution.py:108
  (1 shorter events, 0.0 us)
Async XLA Ops:
  4.0 32.5 %all-to-all-start = ((bf16[16,144,256]{2,1,0:T(8,128)(2,1)}), bf16[16,144,256]{2,1,0:T(8,128)(2,1)S(1)}, u32[]{:S(2)}, u32[]{:S(2)}) async-start(bf16[16,144,256]{2,1,0:T(8,128)(2,1)} %shard_map.163), calls=%async_computation | async-start | bytes 2359296 | tf_op jit(solution)/shard_map/all_to_all | solution.py:447
  36.5 32.6 %all-to-all-start.1 = ((bf16[16,144,256]{2,1,0:T(8,128)(2,1)}), bf16[16,144,256]{2,1,0:T(8,128)(2,1)S(1)}, u32[]{:S(2)}, u32[]{:S(2)}) async-start(bf16[16,144,256]{2,1,0:T(8,128)(2,1)} %get-tuple-element.20), calls=%async_computation.1 | async-start | bytes 2359296 | tf_op jit(solution)/shard_map/all_to_all | solution.py:447
  44.0 10.0 %copy-start.3 = (f32[3,512]{1,0:T(4,128)S(1)}, f32[3,512]{1,0:T(4,128)}, u32[]{:S(2)}) copy-start(f32[3,512]{1,0:T(4,128)} %refs_4_.2) | copy-start | bytes 18436
  50.2 18.9 %collective-permute-start = (bf16[512,512]{1,0:T(8,128)(2,1)}, bf16[512,512]{1,0:T(8,128)(2,1)S(1)}, u32[]{:S(2)}, u32[]{:S(2)}) collective-permute-start(bf16[512,512]{1,0:T(8,128)(2,1)} %get-tuple-element.19.refs_0_), channel_id=1, source_target_pairs={{0,1},{1,2},{2,3},{3,4},{4,5},{5,6},{6,7},{7,8},{8,9},{9,10},{10,1... | collective-permute-start | bytes 1572872 | tf_op jit(solution)/shard_map/ppermute | solution.py:480
  52.5 16.6 %collective-permute-start.1 = (bf16[512,512]{1,0:T(8,128)(2,1)}, bf16[512,512]{1,0:T(8,128)(2,1)S(1)}, u32[]{:S(2)}, u32[]{:S(2)}) collective-permute-start(bf16[512,512]{1,0:T(8,128)(2,1)} %get-tuple-element.19.refs_0_), channel_id=1, source_target_pairs={{1,0},{2,1},{3,2},{4,3},{5,4},{6,5},{7,6},{8,7},{9,8},{10,9},{11,1... | collective-permute-start | bytes 1572872 | tf_op jit(solution)/shard_map/ppermute | solution.py:481
  54.9 14.2 %copy-start.2 = (s32[4,4]{1,0:T(4,128)S(1)}, s32[4,4]{1,0:T(4,128)}, u32[]{:S(2)}) copy-start(s32[4,4]{1,0:T(4,128)} %refs_1_.3) | copy-start | bytes 196
  69.1 38.3 %copy-start = (s32[1024,1]{0,1:T(1,128)S(1)}, s32[1024,1]{0,1:T(1,128)}, u32[]{:S(2)}) copy-start(s32[1024,1]{0,1:T(1,128)} %param.21) | copy-start | bytes 12292
  69.1 38.3 %copy-start.1 = (f32[1,1024]{1,0:T(1,128)S(1)}, f32[1,1024]{1,0:T(1,128)}, u32[]{:S(2)}) copy-start(f32[1,1024]{1,0:T(1,128)} %get-tuple-element.32.refs_1_) | copy-start | bytes 12292

commit v4 on v3

--- a/solution.py
+++ b/solution.py
@@ -10,11 +10,14 @@
 HEADS = 4
 BLK = 128
 NB = 4
-META = 16
+META = 8
 ROWS = 512
-LOW = 32
+LOW = 128
+UPPER = 4
+KEYS_OF = 2
 MASKED = -1e30
 LOG2E = 1.4426950408889634
+PARTS = 4
 VMEM_LIMIT = 24 * 1024 * 1024
 
 epsilon = 1e-05
@@ -62,16 +65,30 @@
         return self.near
 
 
+class Near:
+    def __init__(self, ref):
+        self.near = ref
+
+    def __call__(self):
+        return self.near
+
+    def send(self):
+        pass
+
+
 class Sent:
     def __init__(self, near, far, sem):
-        self.near = near
-        self.copy = pltpu.make_async_copy(near, far, sem)
-        self.started = False
-
-    def send(self):
-        if not self.started:
-            self.copy.start()
-            self.started = True
+        self.near, self.far, self.sem = near, far, sem
+        self.copies = []
+
+    def send(self, n=0, part=None):
+        near, far = (self.near, self.far) if part is None else (self.near.at[part], self.far.at[part])
+        self.copies.append(pltpu.make_async_copy(near, far, self.sem.at[n]))
+        self.copies[-1].start()
+
+    def finish(self):
+        for c in self.copies:
+            c.wait()
 
 
 def call(kernel, outs, args, kinds, scratch=(), late=(), flops=0, moved=0):
@@ -80,22 +97,25 @@
     far_out = [i for i in range(n_out) if outs[i][2] == "H"]
 
     def wrapped(*refs):
-        ins, results = list(refs[:n_in]), list(refs[n_in : n_in + n_out])
+        ins, results = refs[:n_in], refs[n_in : n_in + n_out]
         rest = list(refs[n_in + n_out :])
-        sems = rest.pop(0)
+        sems, out_sems = rest.pop(0), rest.pop(0)
+        ins = [Near(r) if kinds[i] == "V" else r for i, r in enumerate(ins)]
+        results = [Near(r) for r in results]
         for n, i in enumerate(far_in):
-            ins[i] = Held(ins[i], rest.pop(0), sems.at[n])
+            ins[i] = Held(refs[i], rest.pop(0), sems.at[n])
             if i not in late:
                 ins[i].start()
         for n, i in enumerate(far_out):
-            results[i] = Sent(rest.pop(0), results[i], sems.at[len(far_in) + n])
+            results[i] = Sent(rest.pop(0), refs[n_in + i], out_sems.at[n])
         kernel(*ins, *results, *rest)
-        for i in far_out:
-            results[i].send()
         for i in far_in:
             ins[i]()
         for i in far_out:
-            results[i].copy.wait()
+            if not results[i].copies:
+                results[i].send()
+        for i in far_out:
+            results[i].finish()
 
     spaces = {"V": pltpu.VMEM, "H": pltpu.HBM, "S": pltpu.SMEM}
 
@@ -113,7 +133,10 @@
         ),
         in_specs=[spec(kind) for kind in kinds],
         out_specs=tuple(spec(kind) for _, _, kind in outs),
-        scratch_shapes=[pltpu.SemaphoreType.DMA((max(1, len(far_in) + len(far_out)),))]
+        scratch_shapes=[
+            pltpu.SemaphoreType.DMA((max(1, len(far_in)),)),
+            pltpu.SemaphoreType.DMA((max(1, len(far_out)), PARTS)),
+        ]
         + [pltpu.VMEM(args[i].shape, args[i].dtype) for i in far_in]
         + [pltpu.VMEM(outs[i][0], outs[i][1]) for i in far_out]
         + list(scratch),
@@ -138,7 +161,8 @@
     held_weight = refs.pop(0) if weighted else None
     held_rows = refs.pop(0)
     turns = [refs.pop(0) for _ in range(turned)]
-    out, rank_out = refs.pop(0), refs.pop(0) if weighted else None
+    out = refs.pop(0)
+    rank_out, key_out = (refs.pop(0), refs.pop(0)) if weighted else (None, None)
     turned_outs = [refs.pop(0) for _ in range(turned)]
     send_ref = out.near
     grid, width = held_rows.near.shape
@@ -165,11 +189,17 @@
     placed = rank_onehot(rank, cap)
 
     slots = held_slot()[...]
-    pieces = [(slots // LOW).astype(F32), (slots % LOW).astype(F32)]
+    lower = lax.rem(slots, LOW)
+    upper = lax.div(slots, LOW)
+    packed = upper[0:1]
+    for k in range(1, slots.shape[0]):
+        packed = packed + upper[k : k + 1] * UPPER**k
+    pieces = [lower.astype(F32), packed.astype(F32)]
     if weighted:
         pieces.append(held_weight()[...])
     used = sum(p.shape[0] for p in pieces)
-    pieces.append(jnp.zeros((META - used, grid), F32))
+    if used < META:
+        pieces.append(jnp.zeros((META - used, grid), F32))
     features = jnp.concatenate(pieces, axis=0).astype(BF16).astype(F32)
     spread = (chosen[:, None, :] * features[None, :, :]).reshape(peers * META, grid)
     meta = dot_nt(spread.astype(BF16), placed).reshape(peers, META, cap)
@@ -178,16 +208,19 @@
 
     rows = held_rows()[...]
     step = ROWS // cap
-    for o in range(0, peers, step):
+    for n, o in enumerate(range(0, peers, step)):
         select = (chosen16[o : o + step, None, :] * placed[None, :, :]).reshape(step * cap, grid)
         moved = dot(select, rows)
         send_ref[o : o + step, :cap, :] = moved.astype(BF16).reshape(step, cap, width)
-    out.send()
+        out.send(n, pl.ds(o, step))
     for f, t in zip(turns, turned_outs):
         source = f()
         skipped = source.shape[1] - t.near.shape[0]
         t.near[...] = source[:, skipped:].T
         t.send()
+    if weighted:
+        columns = key_out.near.shape[1]
+        key_out.near[...] = turns[KEYS_OF]()[:, columns : 2 * columns]
 
 
 def bucket(owner, slots, weights, rows, turns, peers, cap):
@@ -196,7 +229,8 @@
     args = (owner, slots) + ((weights,) if weighted else ()) + (rows,) + tuple(x for x, _ in turns)
     outs = [((peers, cap + META, width), BF16, "H")]
     if weighted:
-        outs.append(((1, grid), F32, "H"))
+        depth, columns = turns[KEYS_OF][0].shape
+        outs += [((1, grid), F32, "H"), ((depth, columns // 3), BF16, "H")]
     outs += [((count, x.shape[0]), x.dtype, "H") for x, count in turns]
     return call(
         functools.partial(bucket_kernel, peers, cap, weighted, len(turns)),
@@ -215,20 +249,26 @@
     )
 
 
-def slot_row(got_ref, o, step, cap, low, count):
-    return meta_row(got_ref, o, step, cap, low) * LOW + meta_row(
-        got_ref, o, step, cap, low + count
-    )
-
-
-def encode_kernel(peers, cap, got_ref, embed, message_w, state, gain, stream, normed, target_ref, message_ref):
+def slot_rows(got_ref, o, step, cap, count):
+    upper = meta_row(got_ref, o, step, cap, count).astype(jnp.int32)
+    rows = []
+    for k in range(count):
+        rows.append(
+            meta_row(got_ref, o, step, cap, k)
+            + (lax.rem(lax.div(upper, UPPER**k), UPPER) * LOW).astype(F32)
+        )
+    return rows
+
+
+def encode_kernel(peers, cap, got, embed, message_w, state, gain, stream, normed, target_ref, message_ref):
+    got_ref = got()
     width = got_ref.shape[2]
     nodes = stream.near.shape[0]
     step = ROWS // cap
     places = lax.broadcasted_iota(jnp.int32, (nodes, ROWS), 0).astype(F32)
     starts = range(0, peers, step)
     for n, o in enumerate(starts):
-        slot = slot_row(got_ref, o, step, cap, 0, 1)
+        (slot,) = slot_rows(got_ref, o, step, cap, 1)
         target_ref[:, n * ROWS : (n + 1) * ROWS] = jnp.where(places == slot, 1.0, 0.0).astype(BF16)
     embed_ref = embed()
     latents = [
@@ -239,9 +279,9 @@
     for n, latent in enumerate(latents):
         message_ref[n * ROWS : (n + 1) * ROWS, :] = dot(latent, message_w_ref[...]).astype(BF16)
     total = state()[...].astype(F32) + dot(target_ref[...], message_ref[...])
+    stream.near[...] = total
+    stream.send()
     normed.near[...] = layer_norm(total, gain()[0:1, :]).astype(BF16)
-    normed.send()
-    stream.near[...] = total
 
 
 def layer_norm_columns(values, gains):
@@ -280,10 +320,11 @@
     cap,
     where_ref,
     att_ref,
-    before_ref,
-    after_ref,
-    got_ref,
-    qkv,
+    before,
+    after,
+    got,
+    embed_t,
+    key_w,
     value_t,
     query_t,
     stats,
@@ -293,16 +334,16 @@
     up_t,
     down_t,
     gain_t,
-    embed_t,
     dec1_t,
     dec2_t,
-    out_ref,
+    out,
     key_ref,
     value_ref,
     attended_ref,
     mix_ref,
     hidden_ref,
 ):
+    before_ref, after_ref, got_ref, out_ref = before(), after(), got(), out.near
     width, nodes = attended_ref.shape
     head = width // HEADS
     blocks = nodes // BLK
@@ -316,17 +357,24 @@
     places = lax.broadcasted_iota(jnp.int32, (nodes, ROWS), 0).astype(F32)
     for n, o in chunks:
         mix = jnp.zeros((nodes, ROWS), F32)
-        for k in range(3):
-            slot = slot_row(got_ref, o, step, cap, k, 3)
-            weight = meta_row(got_ref, o, step, cap, 6 + k)
+        for k, slot in enumerate(slot_rows(got_ref, o, step, cap, 3)):
+            weight = meta_row(got_ref, o, step, cap, 4 + k)
             mix = mix + jnp.where(places == slot, weight, 0.0)
         mix_ref[n] = mix.astype(BF16)
 
-    qkv_ref, value_t_ref = qkv(), value_t()
+    embed_ref = embed_t()
+    latents = [
+        silu(dot_nt(embed_ref[...], got_ref[o : o + step, :cap, :].reshape(ROWS, columns))).astype(
+            BF16
+        )
+        for _, o in chunks
+    ]
+
+    key_w_ref, value_t_ref = key_w(), value_t()
     for n, side in enumerate((before_ref, after_ref)):
-        key_ref[n * nodes : (n + 1) * nodes, :] = dot(
-            side[...], qkv_ref[:, width : 2 * width]
-        ).astype(BF16)
+        key_ref[n * nodes : (n + 1) * nodes, :] = dot(side[...], key_w_ref[...]).astype(
+            BF16
+        )
         value = dot_nt(value_t_ref[...], side[...]).astype(BF16)
         for i in range(blocks):
             value_ref[n * blocks + i] = value[:, i * BLK : (i + 1) * BLK]
@@ -375,13 +423,7 @@
     stream = stream + dot(down_t()[...], hidden_ref[...])
     final = layer_norm_columns(stream, gains[:, 2:3]).astype(BF16)
 
-    embed_ref, dec1_ref, dec2_ref = embed_t(), dec1_t(), dec2_t()
-    latents = [
-        silu(dot_nt(embed_ref[...], got_ref[o : o + step, :cap, :].reshape(ROWS, columns))).astype(
-            BF16
-        )
-        for _, o in chunks
-    ]
+    dec1_ref, dec2_ref = dec1_t(), dec2_t()
     pulled = [dot(final, mix_ref[n]).astype(BF16) for n, _ in chunks]
     mixed = [
         (latents[n].astype(F32) + pulled[n].astype(F32)).astype(BF16) for n, _ in chunks
@@ -406,14 +448,14 @@
     )
 
 
-def return_kernel(peers, cap, got_ref, rank, owner, out_ref):
-    channels, grid = out_ref.shape
-    placed = rank_onehot(rank[...], cap)
-    chosen = owner_onehot(owner[...], peers)
+def return_kernel(peers, cap, got, rank, owner, out):
+    channels, grid = out.near.shape
+    placed = rank_onehot(rank()[...], cap)
+    chosen = owner_onehot(owner()[...], peers)
     total = jnp.zeros((channels, grid), F32)
     for o in range(peers):
-        total = total + dot(got_ref[o], placed) * chosen[o : o + 1, :]
-    out_ref[...] = total.astype(BF16)
+        total = total + dot(got()[o], placed) * chosen[o : o + 1, :]
+    out.near[...] = total.astype(BF16)
 
 
 def body(
@@ -448,7 +490,7 @@
 
     (enc_send,) = bucket(enc_owner.T, enc_slot.T, None, grid_in, (), peers, cap)
     enc_got = exchange(enc_send)
-    dec_send, rank, embed_t, dec1_t, value_t, out_t, up_t, down_t = bucket(
+    dec_send, rank, key_w, embed_t, dec1_t, value_t, out_t, up_t, down_t = bucket(
         dec_owner.T,
         dec_slot.T,
         dec_weight.T,
@@ -502,7 +544,8 @@
             before,
             after,
             dec_got,
-            w_qkv[0],
+            embed_t,
+            key_w,
             value_t,
             query_t,
             stats,
@@ -512,7 +555,6 @@
             up_t,
             down_t,
             norm_gain.T,
-            embed_t,
             dec1_t,
             w_dec2.T,
         ),

time: 110 us -> 107 us (0.973)
  waiting for transfers between devices: 26.7 us -> 24.5 us
    all_to_all x2, waiting for transfers between devices: 26.7 us -> 24.5 us  [exchange(): return lax.all_to_all(x, 'band', split_axis=0, concat_axis=0, tiled=True)]
  transfers between devices with their start and end apart: 4 -> 4, of which waited for: 2 -> 2; matrix products, arithmetic and copies ran while one was open for 1% -> 1% of each run, Pallas kernels for 17% -> 18%
where the time goes in v4:
time: 107 us; the launch traced here: 106 us
  Pallas kernels  38.5 us (36%)
  waiting for transfers between devices  24.5 us (23%)
  blocking collectives  23.9 us (22%)
  starting transfers between devices  18.4 us (17%)
    pallas_call x6, Pallas kernels, call(): pl.pallas_call(wrapped, out_shape=tuple((pltpu.HBM(shape, dtype) if kind...  38.5 us
    all_to_all x2, waiting for transfers between devices, exchange(): return lax.all_to_all(x, 'band', split_axis=0, concat_axis=0, tiled=True)  24.5 us
    all_to_all x1, blocking collectives, exchange(): return lax.all_to_all(x, 'band', split_axis=0, concat_axis=0, tiled=True)  23.9 us
    all_to_all x2, starting transfers between devices, exchange(): return lax.all_to_all(x, 'band', split_axis=0, concat_axis=0, tiled=True)  14.6 us
    ppermute x1, starting transfers between devices, body(): before = lax.ppermute(normed, 'band', up)  2.34 us
  transfers between devices with their start and end apart: 4, of which 2 were waited for; matrix products, arithmetic and copies ran while one was open for 1% of the time, Pallas kernels for 18%

profile of v4, /device:TPU:0, one launch (start us, length us, event | category | flops | bytes accessed | tf_op | source)
XLA Modules:
  0.0 106.5 jit_solution(932803200352352554)
XLA Ops:
  0.0 3.5 %shard_map.163 = bf16[16,136,256]{2,1,0:T(8,128)(2,1)} custom-call(s32[1,1024]{1,0:T(1,128)} %bitcast.23, s32[1,1024]{1,0:T(1,128)} %bitcast.24, bf16[1024,256]{1,0:T(8,128)(2,1)} %refs_3_.3), custom_call_target="tpu_custom_call" | custom-call | flops 1073741824 | bytes 1638400 | tf_op jit(solution)/shard_map/pallas_call | solution.py:128
  3.6 7.4 %all-to-all-start = ((bf16[16,136,256]{2,1,0:T(8,128)(2,1)}), bf16[16,136,256]{2,1,0:T(8,128)(2,1)S(1)}, u32[]{:S(2)}, u32[]{:S(2)}) async-start(bf16[16,136,256]{2,1,0:T(8,128)(2,1)} %shard_map.163), calls=%async_computation | async-start | bytes 2228224 | tf_op jit(solution)/shard_map/all_to_all | solution.py:489
  10.9 6.6 %shard_map.165 = (bf16[16,136,256]{2,1,0:T(8,128)(2,1)}, f32[1,1024]{1,0:T(1,128)}, bf16[512,512]{1,0:T(8,128)(2,1)}, bf16[512,256]{1,0:T(8,128)(2,1)}, bf16[512...) custom-call(s32[1,1024]{1,0:T(1,128)} %bitcast.12, ...), custom_call_target="tpu_custom_call" | custom-call | flops 1073741824 | bytes 1638400 | tf_op jit(solution)/shard_map/pallas_call | solution.py:128
  17.6 17.4 %all-to-all-done.refs_0_ = bf16[16,136,256]{2,1,0:T(8,128)(2,1)S(1)} async-done(((bf16[16,136,256]{2,1,0:T(8,128)(2,1)}), bf16[16,136,256]{2,1,0:T(8,128)(2,1)S(1)}, u32[]{:S(2)}, u32[]{:S(2)}) %all-to-all-start) | async-done | bytes 1114144 | tf_op jit(solution)/shard_map/all_to_all | solution.py:489
  35.0 7.2 %all-to-all-start.1 = ((bf16[16,136,256]{2,1,0:T(8,128)(2,1)}), bf16[16,136,256]{2,1,0:T(8,128)(2,1)S(1)}, u32[]{:S(2)}, u32[]{:S(2)}) async-start(bf16[16,136,256]{2,1,0:T(8,128)(2,1)} %get-tuple-element.21), calls=%async_computation.1 | async-start | bytes 2228224 | tf_op jit(solution)/shard_map/all_to_all | solution.py:489
  42.1 0.0 copy-start.3
  42.2 5.8 %shard_map.164 = (f32[512,512]{1,0:T(8,128)}, bf16[512,512]{1,0:T(8,128)(2,1)}) custom-call(bf16[16,136,256]{2,1,0:T(8,128)(2,1)S(1)} %all-to-all-done.refs_0_, bf16[256,512]{1,0:T(8,128)(2,1)} %refs_4_.3, bf16[512,512]{1,0:T(8,128)(2,1)} %refs_2_.3, bf16[512,512]{1,0:T(8,128)(2,1)} %refs_3_.2, f32[3,512]{1,0:T(4,128)} %refs_4_.2), custom_call_target="tpu_custom_call" | custom-call | flops 2684354560 | bytes 3145728 | tf_op jit(solution)/shard_map/pallas_call | solution.py:128
  47.9 2.3 %collective-permute-start = (bf16[512,512]{1,0:T(8,128)(2,1)}, bf16[512,512]{1,0:T(8,128)(2,1)S(1)}, u32[]{:S(2)}, u32[]{:S(2)}) collective-permute-start(bf16[512,512]{1,0:T(8,128)(2,1)} %get-tuple-element.20.refs_0_), channel_id=1, source_target_pairs={{0,1},{1,2},{2,3},{3,4},{4,5},{5,6},{6,7},{7,8},{8,9},{9,10},{10,1... | collective-permute-start | bytes 1572872 | tf_op jit(solution)/shard_map/ppermute | solution.py:522
  50.3 1.5 %collective-permute-start.1 = (bf16[512,512]{1,0:T(8,128)(2,1)}, bf16[512,512]{1,0:T(8,128)(2,1)S(1)}, u32[]{:S(2)}, u32[]{:S(2)}) collective-permute-start(bf16[512,512]{1,0:T(8,128)(2,1)} %get-tuple-element.20.refs_0_), channel_id=1, source_target_pairs={{1,0},{2,1},{3,2},{4,3},{5,4},{6,5},{7,6},{8,7},{9,8},{10,9},{11,1... | collective-permute-start | bytes 1572872 | tf_op jit(solution)/shard_map/ppermute | solution.py:523
  51.8 0.0 copy-done.3
  51.8 0.9 copy.18
  52.6 0.1 pad_add_fusion.refs_0_
  52.7 6.4 %shard_map.166 = (bf16[512,512]{1,0:T(8,128)(2,1)}, f32[512,512]{1,0:T(8,128)}, f32[8,512]{1,0:T(8,128)}, f32[512,512]{1,0:T(8,128)}) custom-call(bf16[512,512]{1,0:T(8,128)(2,1)} %get-tuple-element.20.refs_0_, bf16[512,1536]{1,0:T(8,128)(2,1)} %bitcast.17, bf16[512,512]{1,0:T(8,128)(2,1)} %get-tuple-element.24.refs_2_.refs_7_, ...), custom_call_target="tpu_custom_call" | custom-call | flops 1342177280 | bytes 4194304 | tf_op jit(solution)/shard_map/pallas_call | solution.py:128
  59.1 7.1 %all-to-all-done.1.refs_4_ = bf16[16,136,256]{2,1,0:T(8,128)(2,1)S(1)} async-done(((bf16[16,136,256]{2,1,0:T(8,128)(2,1)}), bf16[16,136,256]{2,1,0:T(8,128)(2,1)S(1)}, u32[]{:S(2)}, u32[]{:S(2)}) %all-to-all-start.1) | async-done | bytes 1114144 | tf_op jit(solution)/shard_map/all_to_all | solution.py:489
  66.2 0.0 collective-permute-done.refs_2_
  66.2 0.0 collective-permute-done.1.refs_3_
  66.2 0.0 copy-done.2
  66.2 0.0 copy-start
  66.2 0.0 copy-start.1
  66.2 14.5 %shard_map.167 = bf16[16,84,128]{2,1,0:T(8,128)(2,1)S(1)} custom-call(s32[2]{0:T(128)S(1)} %pad_add_fusion.refs_0_, s32[4,4]{1,0:T(4,128)S(1)} %copy-done.2, bf16[512,512]{1,0:T(8,128)(2,1)S(1)} %collective-permute-done.refs_2_, bf16[512,512]{1,0:T(8,128)(2,1)S(1)} %collective-permute-done.1.refs_3_, bf16[16,136,256]{2,1,0:T(8,128)(2,1)S(1)} %all-to-all-done.1.refs_4_, ...), custom_call_target="tpu_custom_call" | custom-call | flops 6979321856 | bytes 8912896 | tf_op jit(solution)/shard_map/pallas_call | solution.py:128
  80.7 23.9 %all_to_all.15.refs_0_ = bf16[16,84,128]{2,1,0:T(8,128)(2,1)S(1)} all-to-all(bf16[16,84,128]{2,1,0:T(8,128)(2,1)S(1)} %shard_map.167), channel_id=1, replica_groups=mesh['ens'=2,'band'=16] {'band'}, dimensions={0} | all-to-all | bytes 688128 | tf_op jit(solution)/shard_map/all_to_all | solution.py:489
  104.6 0.0 copy-done
  104.6 0.0 copy-done.1
  104.6 1.7 %shard_map.168 = bf16[84,1024]{1,0:T(8,128)(2,1)} custom-call(bf16[16,84,128]{2,1,0:T(8,128)(2,1)S(1)} %all_to_all.15.refs_0_, f32[1,1024]{1,0:T(1,128)S(1)} %copy-done.1, s32[1,1024]{1,0:T(1,128)S(1)} %bitcast.13), custom_call_target="tpu_custom_call" | custom-call | flops 352321536 | bytes 344064 | tf_op jit(solution)/shard_map/pallas_call | solution.py:128
  (1 shorter events, 0.0 us)
Async XLA Ops:
  3.6 31.4 %all-to-all-start = ((bf16[16,136,256]{2,1,0:T(8,128)(2,1)}), bf16[16,136,256]{2,1,0:T(8,128)(2,1)S(1)}, u32[]{:S(2)}, u32[]{:S(2)}) async-start(bf16[16,136,256]{2,1,0:T(8,128)(2,1)} %shard_map.163), calls=%async_computation | async-start | bytes 2228224 | tf_op jit(solution)/shard_map/all_to_all | solution.py:489
  35.0 31.2 %all-to-all-start.1 = ((bf16[16,136,256]{2,1,0:T(8,128)(2,1)}), bf16[16,136,256]{2,1,0:T(8,128)(2,1)S(1)}, u32[]{:S(2)}, u32[]{:S(2)}) async-start(bf16[16,136,256]{2,1,0:T(8,128)(2,1)} %get-tuple-element.21), calls=%async_computation.1 | async-start | bytes 2228224 | tf_op jit(solution)/shard_map/all_to_all | solution.py:489
  42.1 9.6 %copy-start.3 = (f32[3,512]{1,0:T(4,128)S(1)}, f32[3,512]{1,0:T(4,128)}, u32[]{:S(2)}) copy-start(f32[3,512]{1,0:T(4,128)} %refs_4_.2) | copy-start | bytes 18436
  47.9 18.2 %collective-permute-start = (bf16[512,512]{1,0:T(8,128)(2,1)}, bf16[512,512]{1,0:T(8,128)(2,1)S(1)}, u32[]{:S(2)}, u32[]{:S(2)}) collective-permute-start(bf16[512,512]{1,0:T(8,128)(2,1)} %get-tuple-element.20.refs_0_), channel_id=1, source_target_pairs={{0,1},{1,2},{2,3},{3,4},{4,5},{5,6},{6,7},{7,8},{8,9},{9,10},{10,1... | collective-permute-start | bytes 1572872 | tf_op jit(solution)/shard_map/ppermute | solution.py:522
  50.3 15.9 %collective-permute-start.1 = (bf16[512,512]{1,0:T(8,128)(2,1)}, bf16[512,512]{1,0:T(8,128)(2,1)S(1)}, u32[]{:S(2)}, u32[]{:S(2)}) collective-permute-start(bf16[512,512]{1,0:T(8,128)(2,1)} %get-tuple-element.20.refs_0_), channel_id=1, source_target_pairs={{1,0},{2,1},{3,2},{4,3},{5,4},{6,5},{7,6},{8,7},{9,8},{10,9},{11,1... | collective-permute-start | bytes 1572872 | tf_op jit(solution)/shard_map/ppermute | solution.py:523
  52.7 13.5 %copy-start.2 = (s32[4,4]{1,0:T(4,128)S(1)}, s32[4,4]{1,0:T(4,128)}, u32[]{:S(2)}) copy-start(s32[4,4]{1,0:T(4,128)} %refs_1_.3) | copy-start | bytes 196
  66.2 38.4 %copy-start = (s32[1024,1]{0,1:T(1,128)S(1)}, s32[1024,1]{0,1:T(1,128)}, u32[]{:S(2)}) copy-start(s32[1024,1]{0,1:T(1,128)} %param.21) | copy-start | bytes 12292
  66.2 38.4 %copy-start.1 = (f32[1,1024]{1,0:T(1,128)S(1)}, f32[1,1024]{1,0:T(1,128)}, u32[]{:S(2)}) copy-start(f32[1,1024]{1,0:T(1,128)} %get-tuple-element.34.refs_1_) | copy-start | bytes 12292

commit v5 on v4

--- a/solution.py
+++ b/solution.py
@@ -117,10 +117,10 @@
         for i in far_out:
             results[i].finish()
 
-    spaces = {"V": pltpu.VMEM, "H": pltpu.HBM, "S": pltpu.SMEM}
+    spaces = {"V": pltpu.VMEM, "H": pltpu.HBM, "R": pltpu.HBM, "S": pltpu.SMEM}
 
     def spec(kind):
-        return pl.BlockSpec(memory_space=pl.ANY if kind == "H" else spaces[kind])
+        return pl.BlockSpec(memory_space=pl.ANY if kind in "HR" else spaces[kind])
 
     def placed(x, kind):
         return x if kind == "S" else pltpu.with_memory_space_constraint(x, spaces[kind])
@@ -315,6 +315,38 @@
     stream_t.near[...] = stream()[...].T
 
 
+def request_kernel(peers, cap, got, embed_t, *refs):
+    carried = (len(refs) - 3) // 2
+    sources, (mix, latent) = refs[:carried], refs[carried : carried + 2]
+    targets, sems = refs[carried + 2 : -1], refs[-1]
+    copies = [
+        pltpu.make_async_copy(f, t.near, sems.at[n])
+        for n, (f, t) in enumerate(zip(sources, targets))
+    ]
+    for c in copies:
+        c.start()
+    got_ref, mix_ref, latent_ref = got(), mix.near, latent.near
+    nodes = mix_ref.shape[1]
+    columns = got_ref.shape[2]
+    step = ROWS // cap
+    chunks = list(enumerate(range(0, peers, step)))
+
+    places = lax.broadcasted_iota(jnp.int32, (nodes, ROWS), 0).astype(F32)
+    for n, o in chunks:
+        mix = jnp.zeros((nodes, ROWS), F32)
+        for k, slot in enumerate(slot_rows(got_ref, o, step, cap, 3)):
+            weight = meta_row(got_ref, o, step, cap, 4 + k)
+            mix = mix + jnp.where(places == slot, weight, 0.0)
+        mix_ref[n] = mix.astype(BF16)
+
+    embed_ref = embed_t()
+    for n, o in chunks:
+        rows = got_ref[o : o + step, :cap, :].reshape(ROWS, columns)
+        latent_ref[n] = silu(dot_nt(embed_ref[...], rows)).astype(BF16)
+    for c in copies:
+        c.wait()
+
+
 def tail_kernel(
     peers,
     cap,
@@ -322,8 +354,8 @@
     att_ref,
     before,
     after,
-    got,
-    embed_t,
+    mix,
+    latent,
     key_w,
     value_t,
     query_t,
@@ -333,17 +365,17 @@
     out_t,
     up_t,
     down_t,
+    dec1_t,
     gain_t,
-    dec1_t,
     dec2_t,
     out,
     key_ref,
     value_ref,
     attended_ref,
-    mix_ref,
     hidden_ref,
 ):
-    before_ref, after_ref, got_ref, out_ref = before(), after(), got(), out.near
+    before_ref, after_ref, out_ref = before(), after(), out.near
+    mix_ref, latent_ref = mix(), latent()
     width, nodes = attended_ref.shape
     head = width // HEADS
     blocks = nodes // BLK
@@ -351,24 +383,7 @@
     has_before = where_ref[0] > 0
     has_after = where_ref[0] < where_ref[1] - 1
     step = ROWS // cap
-    columns = got_ref.shape[2]
     chunks = list(enumerate(range(0, peers, step)))
-
-    places = lax.broadcasted_iota(jnp.int32, (nodes, ROWS), 0).astype(F32)
-    for n, o in chunks:
-        mix = jnp.zeros((nodes, ROWS), F32)
-        for k, slot in enumerate(slot_rows(got_ref, o, step, cap, 3)):
-            weight = meta_row(got_ref, o, step, cap, 4 + k)
-            mix = mix + jnp.where(places == slot, weight, 0.0)
-        mix_ref[n] = mix.astype(BF16)
-
-    embed_ref = embed_t()
-    latents = [
-        silu(dot_nt(embed_ref[...], got_ref[o : o + step, :cap, :].reshape(ROWS, columns))).astype(
-            BF16
-        )
-        for _, o in chunks
-    ]
 
     key_w_ref, value_t_ref = key_w(), value_t()
     for n, side in enumerate((before_ref, after_ref)):
@@ -426,7 +441,7 @@
     dec1_ref, dec2_ref = dec1_t(), dec2_t()
     pulled = [dot(final, mix_ref[n]).astype(BF16) for n, _ in chunks]
     mixed = [
-        (latents[n].astype(F32) + pulled[n].astype(F32)).astype(BF16) for n, _ in chunks
+        (latent_ref[n].astype(F32) + pulled[n].astype(F32)).astype(BF16) for n, _ in chunks
     ]
     decoded = [silu(dot(dec1_ref[...], mixed[n])).astype(BF16) for n, _ in chunks]
     for n, o in chunks:
@@ -435,15 +450,14 @@
             out_ref[o + r] = result[:, r * cap : (r + 1) * cap]
 
 
-TAIL_KINDS = "SSVVVHHHHHHHHHHHHH"
-
-
-def tail_scratch(nodes, width, slots, hidden):
+TAIL_KINDS = "SSVV" + "V" * 12 + "HH"
+
+
+def tail_scratch(nodes, width, hidden):
     return (
         pltpu.VMEM((2 * nodes, width), BF16),
         pltpu.VMEM((2 * nodes // BLK, width, BLK), BF16),
         pltpu.VMEM((width, nodes), BF16),
-        pltpu.VMEM((slots // ROWS, nodes, ROWS), BF16),
         pltpu.VMEM((hidden, nodes), BF16),
     )
 
@@ -535,31 +549,35 @@
         moved=2 * nodes * width * 8,
     )
     where = jnp.stack([place, jnp.int32(peers)]).astype(jnp.int32)
+    carried = (
+        key_w,
+        value_t,
+        query_t,
+        stats,
+        partial_t,
+        stream_t,
+        out_t,
+        up_t,
+        down_t,
+        dec1_t,
+    )
+    many = (slots // ROWS, width, ROWS)
+    near = call(
+        functools.partial(request_kernel, peers, cap),
+        [((slots // ROWS, nodes, ROWS), BF16, "V"), (many, BF16, "V")]
+        + [(x.shape, x.dtype, "V") for x in carried],
+        (dec_got, embed_t) + carried,
+        "VH" + "R" * len(carried),
+        scratch=(pltpu.SemaphoreType.DMA((len(carried),)),),
+        flops=2 * slots * width * grid_in.shape[1],
+        moved=24 * nodes * width,
+    )
     (result,) = call(
         functools.partial(tail_kernel, peers, cap),
         (((peers, channels, cap), BF16, "V"),),
-        (
-            where,
-            att_list,
-            before,
-            after,
-            dec_got,
-            embed_t,
-            key_w,
-            value_t,
-            query_t,
-            stats,
-            partial_t,
-            stream_t,
-            out_t,
-            up_t,
-            down_t,
-            norm_gain.T,
-            dec1_t,
-            w_dec2.T,
-        ),
+        (where, att_list, before, after, *near, norm_gain.T, w_dec2.T),
         TAIL_KINDS,
-        scratch=tail_scratch(nodes, width, slots, w_up.shape[2]),
+        scratch=tail_scratch(nodes, width, w_up.shape[2]),
         flops=2 * nodes * width * (4 * width + 2 * nodes + width + 2 * w_up.shape[2])
         + 2 * slots * width * (grid_in.shape[1] + nodes + width + 128),
         moved=2 * width * (3 * width + width + 2 * w_up.shape[2]) + 10 * nodes * width,

time: 107 us -> 104 us (0.972)
  blocking collectives: 23.9 us -> 19.8 us
  Pallas kernels: 38.5 us -> 39.6 us
    all_to_all x1, blocking collectives: 23.9 us -> 19.8 us  [exchange(): return lax.all_to_all(x, 'band', split_axis=0, concat_axis=0, tiled=True)]
    pallas_call x6 -> x7, Pallas kernels: 38.5 us -> 39.6 us  [call(): pl.pallas_call(wrapped, out_shape=tuple((pltpu.HBM(shape, dtype) if kind...]
  transfers between devices with their start and end apart: 4 -> 4, of which waited for: 2 -> 2; matrix products, arithmetic and copies ran while one was open for 1% -> 1% of each run, Pallas kernels for 18% -> 22%
where the time goes in v5:
time: 104 us; the launch traced here: 103 us
  Pallas kernels  39.6 us (38%)
  waiting for transfers between devices  24.4 us (23%)
  blocking collectives  19.8 us (19%)
  starting transfers between devices  18.4 us (18%)
    pallas_call x7, Pallas kernels, call(): pl.pallas_call(wrapped, out_shape=tuple((pltpu.HBM(shape, dtype) if kind...  39.6 us
    all_to_all x2, waiting for transfers between devices, exchange(): return lax.all_to_all(x, 'band', split_axis=0, concat_axis=0, tiled=True)  24.4 us
    all_to_all x1, blocking collectives, exchange(): return lax.all_to_all(x, 'band', split_axis=0, concat_axis=0, tiled=True)  19.8 us
    all_to_all x2, starting transfers between devices, exchange(): return lax.all_to_all(x, 'band', split_axis=0, concat_axis=0, tiled=True)  14.6 us
    ppermute x1, starting transfers between devices, body(): before = lax.ppermute(normed, 'band', up)  2.34 us
  transfers between devices with their start and end apart: 4, of which 2 were waited for; matrix products, arithmetic and copies ran while one was open for 1% of the time, Pallas kernels for 22%

profile of v5, /device:TPU:0, one launch (start us, length us, event | category | flops | bytes accessed | tf_op | source)
XLA Modules:
  0.0 103.5 jit_solution(299716104650466261)
XLA Ops:
  0.0 3.6 %shard_map.163 = bf16[16,136,256]{2,1,0:T(8,128)(2,1)} custom-call(s32[1,1024]{1,0:T(1,128)} %bitcast.23, s32[1,1024]{1,0:T(1,128)} %bitcast.24, bf16[1024,256]{1,0:T(8,128)(2,1)} %refs_3_.3), custom_call_target="tpu_custom_call" | custom-call | flops 1073741824 | bytes 1638400 | tf_op jit(solution)/shard_map/pallas_call | solution.py:128
  3.6 7.4 %all-to-all-start = ((bf16[16,136,256]{2,1,0:T(8,128)(2,1)}), bf16[16,136,256]{2,1,0:T(8,128)(2,1)S(1)}, u32[]{:S(2)}, u32[]{:S(2)}) async-start(bf16[16,136,256]{2,1,0:T(8,128)(2,1)} %shard_map.163), calls=%async_computation | async-start | bytes 2228224 | tf_op jit(solution)/shard_map/all_to_all | solution.py:503
  10.9 6.6 %shard_map.165 = (bf16[16,136,256]{2,1,0:T(8,128)(2,1)}, f32[1,1024]{1,0:T(1,128)}, bf16[512,512]{1,0:T(8,128)(2,1)}, bf16[512,256]{1,0:T(8,128)(2,1)}, bf16[512...) custom-call(s32[1,1024]{1,0:T(1,128)} %bitcast.12, ...), custom_call_target="tpu_custom_call" | custom-call | flops 1073741824 | bytes 1638400 | tf_op jit(solution)/shard_map/pallas_call | solution.py:128
  17.6 17.4 %all-to-all-done.refs_0_ = bf16[16,136,256]{2,1,0:T(8,128)(2,1)S(1)} async-done(((bf16[16,136,256]{2,1,0:T(8,128)(2,1)}), bf16[16,136,256]{2,1,0:T(8,128)(2,1)S(1)}, u32[]{:S(2)}, u32[]{:S(2)}) %all-to-all-start) | async-done | bytes 1114144 | tf_op jit(solution)/shard_map/all_to_all | solution.py:503
  35.0 7.2 %all-to-all-start.1 = ((bf16[16,136,256]{2,1,0:T(8,128)(2,1)}), bf16[16,136,256]{2,1,0:T(8,128)(2,1)S(1)}, u32[]{:S(2)}, u32[]{:S(2)}) async-start(bf16[16,136,256]{2,1,0:T(8,128)(2,1)} %get-tuple-element.33), calls=%async_computation.1 | async-start | bytes 2228224 | tf_op jit(solution)/shard_map/all_to_all | solution.py:503
  42.2 0.0 copy-start.3
  42.2 5.9 %shard_map.164 = (f32[512,512]{1,0:T(8,128)}, bf16[512,512]{1,0:T(8,128)(2,1)}) custom-call(bf16[16,136,256]{2,1,0:T(8,128)(2,1)S(1)} %all-to-all-done.refs_0_, bf16[256,512]{1,0:T(8,128)(2,1)} %refs_4_.3, bf16[512,512]{1,0:T(8,128)(2,1)} %refs_2_.3, bf16[512,512]{1,0:T(8,128)(2,1)} %refs_3_.2, f32[3,512]{1,0:T(4,128)} %refs_4_.2), custom_call_target="tpu_custom_call" | custom-call | flops 2684354560 | bytes 3145728 | tf_op jit(solution)/shard_map/pallas_call | solution.py:128
  48.0 2.3 %collective-permute-start = (bf16[512,512]{1,0:T(8,128)(2,1)}, bf16[512,512]{1,0:T(8,128)(2,1)S(1)}, u32[]{:S(2)}, u32[]{:S(2)}) collective-permute-start(bf16[512,512]{1,0:T(8,128)(2,1)} %get-tuple-element.32.refs_0_), channel_id=1, source_target_pairs={{0,1},{1,2},{2,3},{3,4},{4,5},{5,6},{6,7},{7,8},{8,9},{9,10},{10,1... | collective-permute-start | bytes 1572872 | tf_op jit(solution)/shard_map/ppermute | solution.py:536
  50.4 1.5 %collective-permute-start.1 = (bf16[512,512]{1,0:T(8,128)(2,1)}, bf16[512,512]{1,0:T(8,128)(2,1)S(1)}, u32[]{:S(2)}, u32[]{:S(2)}) collective-permute-start(bf16[512,512]{1,0:T(8,128)(2,1)} %get-tuple-element.32.refs_0_), channel_id=1, source_target_pairs={{1,0},{2,1},{3,2},{4,3},{5,4},{6,5},{7,6},{8,7},{9,8},{10,9},{11,1... | collective-permute-start | bytes 1572872 | tf_op jit(solution)/shard_map/ppermute | solution.py:537
  51.9 0.0 copy-done.3
  51.9 0.9 copy.18
  52.7 0.1 pad_add_fusion.refs_0_
  52.8 6.4 %shard_map.166 = (bf16[512,512]{1,0:T(8,128)(2,1)}, f32[512,512]{1,0:T(8,128)}, f32[8,512]{1,0:T(8,128)}, f32[512,512]{1,0:T(8,128)}) custom-call(bf16[512,512]{1,0:T(8,128)(2,1)} %get-tuple-element.32.refs_0_, bf16[512,1536]{1,0:T(8,128)(2,1)} %bitcast.17, bf16[512,512]{1,0:T(8,128)(2,1)} %get-tuple-element.36.refs_2_.refs_3_, ...), custom_call_target="tpu_custom_call" | custom-call | flops 1342177280 | bytes 4194304 | tf_op jit(solution)/shard_map/pallas_call | solution.py:128
  59.2 7.0 %all-to-all-done.1.refs_0_ = bf16[16,136,256]{2,1,0:T(8,128)(2,1)S(1)} async-done(((bf16[16,136,256]{2,1,0:T(8,128)(2,1)}), bf16[16,136,256]{2,1,0:T(8,128)(2,1)S(1)}, u32[]{:S(2)}, u32[]{:S(2)}) %all-to-all-start.1) | async-done | bytes 1114144 | tf_op jit(solution)/shard_map/all_to_all | solution.py:503
  66.2 4.0 %shard_map.167 = (bf16[4,512,512]{2,1,0:T(8,128)(2,1)S(1)}, bf16[4,512,512]{2,1,0:T(8,128)(2,1)S(1)}, bf16[512,512]{1,0:T(8,128)(2,1)S(1)}, bf16[512,512]{1,0:T(...) custom-call(bf16[16,136,256]{2,1,0:T(8,128)(2,1)S(1)} %all-to-all-do, ...), custom_call_target="tpu_custom_call" | custom-call | flops 536870912 | bytes 6291456 | tf_op jit(solution)/shard_map/pallas_call | solution.py:128
  70.2 0.0 collective-permute-done.refs_2_
  70.2 0.0 collective-permute-done.1.refs_3_
  70.2 0.0 copy-done.2
  70.3 0.0 copy-start
  70.3 0.0 copy-start.1
  70.3 11.5 %shard_map.168 = bf16[16,84,128]{2,1,0:T(8,128)(2,1)S(1)} custom-call(s32[2]{0:T(128)S(1)} %pad_add_fusion.refs_0_, s32[4,4]{1,0:T(4,128)S(1)} %copy-done.2, bf16[512,512]{1,0:T(8,128)(2,1)S(1)} %collective-permute-done.refs_2_, bf16[512,512]{1,0:T(8,128)(2,1)S(1)} %collective-permute-done.1.refs_3_, bf16[4,512,512]{2,1,0:T(8,128)(2,1)S(1)} %get-tuple-element.46.refs_4_, ...), custom_call_target="tpu_custom_call" | custom-call | flops 6979321856 | bytes 8912896 | tf_op jit(solution)/shard_map/pallas_call | solution.py:128
  81.8 19.8 %all_to_all.15.refs_0_ = bf16[16,84,128]{2,1,0:T(8,128)(2,1)S(1)} all-to-all(bf16[16,84,128]{2,1,0:T(8,128)(2,1)S(1)} %shard_map.168), channel_id=1, replica_groups=mesh['ens'=2,'band'=16] {'band'}, dimensions={0} | all-to-all | bytes 688128 | tf_op jit(solution)/shard_map/all_to_all | solution.py:503
  101.6 0.0 copy-done
  101.6 1.7 %shard_map.169 = bf16[84,1024]{1,0:T(8,128)(2,1)} custom-call(bf16[16,84,128]{2,1,0:T(8,128)(2,1)S(1)} %all_to_all.15.refs_0_, f32[1,1024]{1,0:T(1,128)S(1)} %copy-done.1, s32[1,1024]{1,0:T(1,128)S(1)} %bitcast.13), custom_call_target="tpu_custom_call" | custom-call | flops 352321536 | bytes 344064 | tf_op jit(solution)/shard_map/pallas_call | solution.py:128
  (2 shorter events, 0.0 us)
Async XLA Ops:
  3.6 31.4 %all-to-all-start = ((bf16[16,136,256]{2,1,0:T(8,128)(2,1)}), bf16[16,136,256]{2,1,0:T(8,128)(2,1)S(1)}, u32[]{:S(2)}, u32[]{:S(2)}) async-start(bf16[16,136,256]{2,1,0:T(8,128)(2,1)} %shard_map.163), calls=%async_computation | async-start | bytes 2228224 | tf_op jit(solution)/shard_map/all_to_all | solution.py:503
  35.0 31.2 %all-to-all-start.1 = ((bf16[16,136,256]{2,1,0:T(8,128)(2,1)}), bf16[16,136,256]{2,1,0:T(8,128)(2,1)S(1)}, u32[]{:S(2)}, u32[]{:S(2)}) async-start(bf16[16,136,256]{2,1,0:T(8,128)(2,1)} %get-tuple-element.33), calls=%async_computation.1 | async-start | bytes 2228224 | tf_op jit(solution)/shard_map/all_to_all | solution.py:503
  42.2 9.7 %copy-start.3 = (f32[3,512]{1,0:T(4,128)S(1)}, f32[3,512]{1,0:T(4,128)}, u32[]{:S(2)}) copy-start(f32[3,512]{1,0:T(4,128)} %refs_4_.2) | copy-start | bytes 18436
  48.0 22.2 %collective-permute-start = (bf16[512,512]{1,0:T(8,128)(2,1)}, bf16[512,512]{1,0:T(8,128)(2,1)S(1)}, u32[]{:S(2)}, u32[]{:S(2)}) collective-permute-start(bf16[512,512]{1,0:T(8,128)(2,1)} %get-tuple-element.32.refs_0_), channel_id=1, source_target_pairs={{0,1},{1,2},{2,3},{3,4},{4,5},{5,6},{6,7},{7,8},{8,9},{9,10},{10,1... | collective-permute-start | bytes 1572872 | tf_op jit(solution)/shard_map/ppermute | solution.py:536
  50.4 19.9 %collective-permute-start.1 = (bf16[512,512]{1,0:T(8,128)(2,1)}, bf16[512,512]{1,0:T(8,128)(2,1)S(1)}, u32[]{:S(2)}, u32[]{:S(2)}) collective-permute-start(bf16[512,512]{1,0:T(8,128)(2,1)} %get-tuple-element.32.refs_0_), channel_id=1, source_target_pairs={{1,0},{2,1},{3,2},{4,3},{5,4},{6,5},{7,6},{8,7},{9,8},{10,9},{11,1... | collective-permute-start | bytes 1572872 | tf_op jit(solution)/shard_map/ppermute | solution.py:537
  66.2 4.1 %copy-start.2 = (s32[4,4]{1,0:T(4,128)S(1)}, s32[4,4]{1,0:T(4,128)}, u32[]{:S(2)}) copy-start(s32[4,4]{1,0:T(4,128)} %refs_1_.3) | copy-start | bytes 196
  70.3 31.3 %copy-start = (s32[1024,1]{0,1:T(1,128)S(1)}, s32[1024,1]{0,1:T(1,128)}, u32[]{:S(2)}) copy-start(s32[1024,1]{0,1:T(1,128)} %param.21) | copy-start | bytes 12292
  70.3 31.3 %copy-start.1 = (f32[1,1024]{1,0:T(1,128)S(1)}, f32[1,1024]{1,0:T(1,128)}, u32[]{:S(2)}) copy-start(f32[1,1024]{1,0:T(1,128)} %get-tuple-element.58.refs_1_) | copy-start | bytes 12292

commit v6 on v5

--- a/solution.py
+++ b/solution.py
@@ -72,7 +72,7 @@
     def __call__(self):
         return self.near
 
-    def send(self):
+    def send(self, n=0, part=None):
         pass
 
 
@@ -227,7 +227,7 @@
     grid, width = rows.shape
     weighted = weights is not None
     args = (owner, slots) + ((weights,) if weighted else ()) + (rows,) + tuple(x for x, _ in turns)
-    outs = [((peers, cap + META, width), BF16, "H")]
+    outs = [((peers, cap + META, width), BF16, "V")]
     if weighted:
         depth, columns = turns[KEYS_OF][0].shape
         outs += [((1, grid), F32, "H"), ((depth, columns // 3), BF16, "H")]
@@ -447,7 +447,7 @@
     for n, o in chunks:
         result = dot(dec2_ref[...], decoded[n]).astype(BF16)
         for r in range(step):
-            out_ref[o + r] = result[:, r * cap : (r + 1) * cap]
+            out_ref[o + r] = result[: out_ref.shape[1], r * cap : (r + 1) * cap]
 
 
 TAIL_KINDS = "SSVV" + "V" * 12 + "HH"
@@ -561,6 +561,7 @@
         down_t,
         dec1_t,
     )
+    dec2_t = jnp.pad(w_dec2.T, ((0, -channels % 16), (0, 0)))
     many = (slots // ROWS, width, ROWS)
     near = call(
         functools.partial(request_kernel, peers, cap),
@@ -575,7 +576,7 @@
     (result,) = call(
         functools.partial(tail_kernel, peers, cap),
         (((peers, channels, cap), BF16, "V"),),
-        (where, att_list, before, after, *near, norm_gain.T, w_dec2.T),
+        (where, att_list, before, after, *near, norm_gain.T, dec2_t),
         TAIL_KINDS,
         scratch=tail_scratch(nodes, width, w_up.shape[2]),
         flops=2 * nodes * width * (4 * width + 2 * nodes + width + 2 * w_up.shape[2])

time: 104 us -> 104 us (level)
  waiting for transfers between devices: 24.4 us -> 22.8 us
  Pallas kernels: 39.6 us -> 40.8 us
    all_to_all x2, waiting for transfers between devices: 24.4 us -> 22.8 us  [exchange(): return lax.all_to_all(x, 'band', split_axis=0, concat_axis=0, tiled=True)]
    pallas_call x7, Pallas kernels: 39.6 us -> 40.8 us  [call(): pl.pallas_call(wrapped, out_shape=tuple((pltpu.HBM(shape, dtype) if kind...]
  transfers between devices with their start and end apart: 4 -> 4, of which waited for: 2 -> 2; matrix products, arithmetic and copies ran while one was open for 1% -> 2% of each run, Pallas kernels for 22% -> 23%
where the time goes in v6:
time: 104 us
  Pallas kernels  40.8 us (39%)
  waiting for transfers between devices  22.8 us (22%)
  blocking collectives  19.8 us (19%)
  starting transfers between devices  18.4 us (18%)
  local copies, waits for them, and re-layouts  1.54 us (1%)
    pallas_call x7, Pallas kernels, call(): pl.pallas_call(wrapped, out_shape=tuple((pltpu.HBM(shape, dtype) if kind...  40.8 us
    all_to_all x2, waiting for transfers between devices, exchange(): return lax.all_to_all(x, 'band', split_axis=0, concat_axis=0, tiled=True)  22.8 us
    all_to_all x1, blocking collectives, exchange(): return lax.all_to_all(x, 'band', split_axis=0, concat_axis=0, tiled=True)  19.8 us
    all_to_all x2, starting transfers between devices, exchange(): return lax.all_to_all(x, 'band', split_axis=0, concat_axis=0, tiled=True)  14.6 us
    ppermute x1, starting transfers between devices, body(): before = lax.ppermute(normed, 'band', up)  2.34 us
  transfers between devices with their start and end apart: 4, of which 2 were waited for; matrix products, arithmetic and copies ran while one was open for 2% of the time, Pallas kernels for 23%

profile of v6, /device:TPU:0, one launch (start us, length us, event | category | flops | bytes accessed | tf_op | source)
XLA Modules:
  0.0 103.7 jit_solution(13437619997434951071)
XLA Ops:
  0.0 3.8 %shard_map.163 = bf16[16,136,256]{2,1,0:T(8,128)(2,1)} custom-call(s32[1,1024]{1,0:T(1,128)} %bitcast.23, s32[1,1024]{1,0:T(1,128)} %bitcast.24, bf16[1024,256]{1,0:T(8,128)(2,1)} %refs_3_.3), custom_call_target="tpu_custom_call" | custom-call | flops 1073741824 | bytes 1638400 | tf_op jit(solution)/shard_map/pallas_call | solution.py:128
  3.8 7.4 %all-to-all-start = ((bf16[16,136,256]{2,1,0:T(8,128)(2,1)}), bf16[16,136,256]{2,1,0:T(8,128)(2,1)S(1)}, u32[]{:S(2)}, u32[]{:S(2)}) async-start(bf16[16,136,256]{2,1,0:T(8,128)(2,1)} %shard_map.163), calls=%async_computation | async-start | bytes 2228224 | tf_op jit(solution)/shard_map/all_to_all | solution.py:503
  11.1 7.5 %shard_map.165 = (bf16[16,136,256]{2,1,0:T(8,128)(2,1)}, f32[1,1024]{1,0:T(1,128)}, bf16[512,512]{1,0:T(8,128)(2,1)}, bf16[512,256]{1,0:T(8,128)(2,1)}, bf16[512...) custom-call(s32[1,1024]{1,0:T(1,128)} %bitcast.12, ...), custom_call_target="tpu_custom_call" | custom-call | flops 1073741824 | bytes 1638400 | tf_op jit(solution)/shard_map/pallas_call | solution.py:128
  18.7 16.5 %all-to-all-done.refs_0_ = bf16[16,136,256]{2,1,0:T(8,128)(2,1)S(1)} async-done(((bf16[16,136,256]{2,1,0:T(8,128)(2,1)}), bf16[16,136,256]{2,1,0:T(8,128)(2,1)S(1)}, u32[]{:S(2)}, u32[]{:S(2)}) %all-to-all-start) | async-done | bytes 1114144 | tf_op jit(solution)/shard_map/all_to_all | solution.py:503
  35.2 7.2 %all-to-all-start.1 = ((bf16[16,136,256]{2,1,0:T(8,128)(2,1)}), bf16[16,136,256]{2,1,0:T(8,128)(2,1)S(1)}, u32[]{:S(2)}, u32[]{:S(2)}) async-start(bf16[16,136,256]{2,1,0:T(8,128)(2,1)} %get-tuple-element.33), calls=%async_computation.1 | async-start | bytes 2228224 | tf_op jit(solution)/shard_map/all_to_all | solution.py:503
  42.4 0.0 copy-start.4
  42.4 0.0 copy-start.3
  42.4 5.9 %shard_map.164 = (f32[512,512]{1,0:T(8,128)}, bf16[512,512]{1,0:T(8,128)(2,1)}) custom-call(bf16[16,136,256]{2,1,0:T(8,128)(2,1)S(1)} %all-to-all-done.refs_0_, bf16[256,512]{1,0:T(8,128)(2,1)} %refs_4_.3, bf16[512,512]{1,0:T(8,128)(2,1)} %refs_2_.3, bf16[512,512]{1,0:T(8,128)(2,1)} %refs_3_.2, f32[3,512]{1,0:T(4,128)} %refs_4_.2), custom_call_target="tpu_custom_call" | custom-call | flops 2684354560 | bytes 3145728 | tf_op jit(solution)/shard_map/pallas_call | solution.py:128
  48.3 2.3 %collective-permute-start = (bf16[512,512]{1,0:T(8,128)(2,1)}, bf16[512,512]{1,0:T(8,128)(2,1)S(1)}, u32[]{:S(2)}, u32[]{:S(2)}) collective-permute-start(bf16[512,512]{1,0:T(8,128)(2,1)} %get-tuple-element.32.refs_0_), channel_id=1, source_target_pairs={{0,1},{1,2},{2,3},{3,4},{4,5},{5,6},{6,7},{7,8},{8,9},{9,10},{10,1... | collective-permute-start | bytes 1572872 | tf_op jit(solution)/shard_map/ppermute | solution.py:536
  50.6 1.5 %collective-permute-start.1 = (bf16[512,512]{1,0:T(8,128)(2,1)}, bf16[512,512]{1,0:T(8,128)(2,1)S(1)}, u32[]{:S(2)}, u32[]{:S(2)}) collective-permute-start(bf16[512,512]{1,0:T(8,128)(2,1)} %get-tuple-element.32.refs_0_), channel_id=1, source_target_pairs={{1,0},{2,1},{3,2},{4,3},{5,4},{6,5},{7,6},{8,7},{9,8},{10,9},{11,1... | collective-permute-start | bytes 1572872 | tf_op jit(solution)/shard_map/ppermute | solution.py:537
  52.1 0.0 copy-done.4
  52.1 0.9 copy.18
  53.0 0.0 copy-done.3
  53.0 0.6 pad.4.refs_17_
  53.6 0.1 pad_add_fusion.refs_0_
  53.7 6.4 %shard_map.166 = (bf16[512,512]{1,0:T(8,128)(2,1)}, f32[512,512]{1,0:T(8,128)}, f32[8,512]{1,0:T(8,128)}, f32[512,512]{1,0:T(8,128)}) custom-call(bf16[512,512]{1,0:T(8,128)(2,1)} %get-tuple-element.32.refs_0_, bf16[512,1536]{1,0:T(8,128)(2,1)} %bitcast.17, bf16[512,512]{1,0:T(8,128)(2,1)} %get-tuple-element.36.refs_2_.refs_3_, ...), custom_call_target="tpu_custom_call" | custom-call | flops 1342177280 | bytes 4194304 | tf_op jit(solution)/shard_map/pallas_call | solution.py:128
  60.1 6.3 %all-to-all-done.1.refs_0_ = bf16[16,136,256]{2,1,0:T(8,128)(2,1)S(1)} async-done(((bf16[16,136,256]{2,1,0:T(8,128)(2,1)}), bf16[16,136,256]{2,1,0:T(8,128)(2,1)S(1)}, u32[]{:S(2)}, u32[]{:S(2)}) %all-to-all-start.1) | async-done | bytes 1114144 | tf_op jit(solution)/shard_map/all_to_all | solution.py:503
  66.4 4.0 %shard_map.167 = (bf16[4,512,512]{2,1,0:T(8,128)(2,1)S(1)}, bf16[4,512,512]{2,1,0:T(8,128)(2,1)S(1)}, bf16[512,512]{1,0:T(8,128)(2,1)S(1)}, bf16[512,512]{1,0:T(...) custom-call(bf16[16,136,256]{2,1,0:T(8,128)(2,1)S(1)} %all-to-all-do, ...), custom_call_target="tpu_custom_call" | custom-call | flops 536870912 | bytes 6291456 | tf_op jit(solution)/shard_map/pallas_call | solution.py:128
  70.4 0.0 collective-permute-done.refs_2_
  70.4 0.0 collective-permute-done.1.refs_3_
  70.5 0.0 copy-start
  70.5 11.5 %shard_map.168 = bf16[16,84,128]{2,1,0:T(8,128)(2,1)S(1)} custom-call(s32[2]{0:T(128)S(1)} %pad_add_fusion.refs_0_, s32[4,4]{1,0:T(4,128)S(1)} %copy-done.2, bf16[512,512]{1,0:T(8,128)(2,1)S(1)} %collective-permute-done.refs_2_, bf16[512,512]{1,0:T(8,128)(2,1)S(1)} %collective-permute-done.1.refs_3_, bf16[4,512,512]{2,1,0:T(8,128)(2,1)S(1)} %get-tuple-element.46.refs_4_, ...), custom_call_target="tpu_custom_call" | custom-call | flops 6979321856 | bytes 8912896 | tf_op jit(solution)/shard_map/pallas_call | solution.py:128
  82.0 19.8 %all_to_all.15.refs_0_ = bf16[16,84,128]{2,1,0:T(8,128)(2,1)S(1)} all-to-all(bf16[16,84,128]{2,1,0:T(8,128)(2,1)S(1)} %shard_map.168), channel_id=1, replica_groups=mesh['ens'=2,'band'=16] {'band'}, dimensions={0} | all-to-all | bytes 688128 | tf_op jit(solution)/shard_map/all_to_all | solution.py:503
  101.9 1.7 %shard_map.169 = bf16[84,1024]{1,0:T(8,128)(2,1)} custom-call(bf16[16,84,128]{2,1,0:T(8,128)(2,1)S(1)} %all_to_all.15.refs_0_, f32[1,1024]{1,0:T(1,128)S(1)} %copy-done.1, s32[1,1024]{1,0:T(1,128)S(1)} %bitcast.13), custom_call_target="tpu_custom_call" | custom-call | flops 352321536 | bytes 344064 | tf_op jit(solution)/shard_map/pallas_call | solution.py:128
  (5 shorter events, 0.0 us)
Async XLA Ops:
  3.8 31.4 %all-to-all-start = ((bf16[16,136,256]{2,1,0:T(8,128)(2,1)}), bf16[16,136,256]{2,1,0:T(8,128)(2,1)S(1)}, u32[]{:S(2)}, u32[]{:S(2)}) async-start(bf16[16,136,256]{2,1,0:T(8,128)(2,1)} %shard_map.163), calls=%async_computation | async-start | bytes 2228224 | tf_op jit(solution)/shard_map/all_to_all | solution.py:503
  35.2 31.2 %all-to-all-start.1 = ((bf16[16,136,256]{2,1,0:T(8,128)(2,1)}), bf16[16,136,256]{2,1,0:T(8,128)(2,1)S(1)}, u32[]{:S(2)}, u32[]{:S(2)}) async-start(bf16[16,136,256]{2,1,0:T(8,128)(2,1)} %get-tuple-element.33), calls=%async_computation.1 | async-start | bytes 2228224 | tf_op jit(solution)/shard_map/all_to_all | solution.py:503
  42.4 9.7 %copy-start.4 = (f32[3,512]{1,0:T(4,128)S(1)}, f32[3,512]{1,0:T(4,128)}, u32[]{:S(2)}) copy-start(f32[3,512]{1,0:T(4,128)} %refs_4_.2) | copy-start | bytes 18436
  42.4 10.6 %copy-start.3 = (bf16[512,84]{0,1:T(8,128)(2,1)S(1)}, bf16[512,84]{0,1:T(8,128)(2,1)}, u32[]{:S(2)}) copy-start(bf16[512,84]{0,1:T(8,128)(2,1)} %param.33) | copy-start | bytes 258052
  48.3 22.2 %collective-permute-start = (bf16[512,512]{1,0:T(8,128)(2,1)}, bf16[512,512]{1,0:T(8,128)(2,1)S(1)}, u32[]{:S(2)}, u32[]{:S(2)}) collective-permute-start(bf16[512,512]{1,0:T(8,128)(2,1)} %get-tuple-element.32.refs_0_), channel_id=1, source_target_pairs={{0,1},{1,2},{2,3},{3,4},{4,5},{5,6},{6,7},{7,8},{8,9},{9,10},{10,1... | collective-permute-start | bytes 1572872 | tf_op jit(solution)/shard_map/ppermute | solution.py:536
  50.6 19.8 %collective-permute-start.1 = (bf16[512,512]{1,0:T(8,128)(2,1)}, bf16[512,512]{1,0:T(8,128)(2,1)S(1)}, u32[]{:S(2)}, u32[]{:S(2)}) collective-permute-start(bf16[512,512]{1,0:T(8,128)(2,1)} %get-tuple-element.32.refs_0_), channel_id=1, source_target_pairs={{1,0},{2,1},{3,2},{4,3},{5,4},{6,5},{7,6},{8,7},{9,8},{10,9},{11,1... | collective-permute-start | bytes 1572872 | tf_op jit(solution)/shard_map/ppermute | solution.py:537
  66.4 4.1 %copy-start.2 = (s32[4,4]{1,0:T(4,128)S(1)}, s32[4,4]{1,0:T(4,128)}, u32[]{:S(2)}) copy-start(s32[4,4]{1,0:T(4,128)} %refs_1_.3) | copy-start | bytes 196
  70.5 31.4 %copy-start = (s32[1024,1]{0,1:T(1,128)S(1)}, s32[1024,1]{0,1:T(1,128)}, u32[]{:S(2)}) copy-start(s32[1024,1]{0,1:T(1,128)} %param.21) | copy-start | bytes 12292
  70.5 31.4 %copy-start.1 = (f32[1,1024]{1,0:T(1,128)S(1)}, f32[1,1024]{1,0:T(1,128)}, u32[]{:S(2)}) copy-start(f32[1,1024]{1,0:T(1,128)} %get-tuple-element.58.refs_1_) | copy-start | bytes 12292
